TPU v7x, 32 devices: a whole 2x2x4 slice. The times are simulated.
32 devices in a mesh: groups: 2 (over y), replica: 2 (over core), tensor: 8 (over z, x).
Axes of the slice: x: 2, y: 2, z: 4, core: 2. Of those that a mesh axis runs over, the one named last changes fastest.
Arguments:
- acts: bfloat16 [256, 8192], P(('groups', 'replica'), 'tensor'), parts along dimension 0, may hold values from -6 to 6
- base_output_matrix: bfloat16 [8192, 8192], P('tensor'), may hold values from -0.09375 to 0.09375
- stored_down_factors: bfloat16 [256, 8192, 64], P('replica', 'tensor'), may hold values from -0.0625 to 0.0625
- stored_up_factors: bfloat16 [256, 64, 8192], P('replica', None, 'tensor'), may hold values from -0.75 to 0.75
- adapter_storage_row: int32 [256], replicated, may hold values from 0 to 255, each once
- adapter_per_block: int32 [16], P(('groups', 'replica')), parts along dimension 0, may hold values from 0 to 255, as said below
- adapter_per_token: int32 [256], P(('groups', 'replica')), parts along dimension 0, may hold values from -1 to 255, as said below
Outputs:
- projected: bfloat16 [256, 8192], P(('groups', 'replica'), 'tensor'), parts along dimension 0
There are 2 independent parts, one for each index of `groups`. A program takes and returns all parts, laid end to end along the dimension named above; an argument that names none is the same for every part. Nothing has to cross between parts.
Inputs may be any that keep to these rules, and one draw needn't show every extreme that they name: A permutation: adapter a is stored at row adapter_storage_row[a] of stored_down_factors and stored_up_factors, so by replica adapter_storage_row[a] // 128. `adapter_per_block`: the adapter of each aligned block of 16 token rows. `adapter_per_token`: in each aligned block of 16 token rows, the first rows (one or more) hold that block's entry of adapter_per_block and the rest hold -1.
All inputs are finite; a program needn't handle non-finite values.
Results may differ from a plain program's by a relative error of at most 0.001.
Values may be sent and summed in bfloat16 or wider, within the bound.
A program may use at most 128 MiB of HBM per device.

v0:
```python
import jax
import jax.numpy as jnp
from jax import lax
from jax.sharding import PartitionSpec as P


def shards(
    acts,
    base_output_matrix,
    stored_down_factors,
    stored_up_factors,
    adapter_storage_row,
    adapter_per_block,
    adapter_per_token,
):
    tok_rows, feature_list = acts.shape
    owned_adapters = stored_down_factors.shape[0]
    rank_value = stored_down_factors.shape[2]
    block_count = adapter_per_block.shape[0]
    block_rows = tok_rows // block_count
    replica_count = lax.axis_size("replica")
    my_rows = adapter_storage_row[adapter_per_block]
    wanted = lax.all_gather(adapter_per_block, "replica", axis=0, tiled=True)
    stored = adapter_storage_row[wanted]
    holder = stored // owned_adapters
    local_row_index = stored % owned_adapters
    local_adapters = (holder == lax.axis_index("replica"))[:, None, None]
    zero_value = jnp.zeros((), jnp.bfloat16)
    outgoing_down = jnp.where(
        local_adapters, stored_down_factors[local_row_index], zero_value
    ).reshape(replica_count, block_count, feature_list, rank_value)
    outgoing_up = jnp.where(local_adapters, stored_up_factors[local_row_index], zero_value).reshape(
        replica_count, block_count, rank_value, stored_up_factors.shape[2]
    )
    got_down, got_up = (
        lax.all_to_all(outgoing_down, "replica", split_axis=0, concat_axis=0, tiled=True),
        lax.all_to_all(outgoing_up, "replica", split_axis=0, concat_axis=0, tiled=True),
    )
    source = my_rows // owned_adapters
    picked = (jnp.arange(replica_count, dtype=jnp.int32)[:, None] == source[None, :])[
        :, :, None, None
    ]
    fetched_down = jnp.sum(jnp.where(picked, got_down, zero_value), axis=0)
    fetched_up = jnp.sum(jnp.where(picked, got_up, zero_value), axis=0)
    alive = (adapter_per_token >= 0).astype(jnp.float32).reshape(block_count, block_rows, 1)
    grouped = acts.reshape(block_count, block_rows, feature_list)
    shrunk_part = (
        jnp.einsum("bkf,bfr->bkr", grouped, fetched_down, preferred_element_type=jnp.float32)
        * alive
    )
    piece = lax.all_gather(fetched_up, "tensor", axis=2, tiled=True)
    width = piece.shape[2]
    part_base = jnp.dot(acts, base_output_matrix, preferred_element_type=jnp.float32)
    part_delta = jnp.einsum(
        "bkr,brc->bkc", shrunk_part, piece.astype(jnp.float32), precision=lax.Precision.HIGHEST
    )
    partial_value = part_base + part_delta.reshape(tok_rows, width)
    total = lax.psum_scatter(partial_value, "tensor", scatter_dimension=1, tiled=True)
    return total.astype(jnp.bfloat16)


def solution(mesh):
    placed = (
        P(("groups", "replica"), "tensor"),
        P("tensor", None),
        P("replica", "tensor", None),
        P("replica", None, "tensor"),
        P(),
        P(("groups", "replica")),
        P(("groups", "replica")),
    )
    return jax.shard_map(
        shards,
        mesh=mesh,
        in_specs=placed,
        out_specs=P(("groups", "replica"), "tensor"),
        check_vma=False,
    )
```

profile of v0, /device:TPU:0, one launch (start us, length us, event | category | flops | bytes accessed | tf_op | source)
XLA Modules:
  0.0 192.1 jit_solution(7565747633940547764)
XLA Ops:
  6.5 1.3 dynamic-slice
  8.5 0.9 dynamic-update-slice
  9.3 1.9 %all-reduce = s32[8]{0:T(128)S(1)} all-reduce(s32[8]{0:T(128)S(1)} %dynamic-update-slice), channel_id=1, replica_groups=mesh['groups'=2,'replica'=2,'tensor'=8] {'replica'}, use_global_device_ids=true, to_apply=%add | all-reduce | flops 8 | bytes 64
  11.3 1.3 gather_fusion.1
  12.6 0.1 gather.22
  12.7 6.4 %gather_fusion.3 = bf16[8,64,1024]{2,1,0:T(8,128)(2,1)S(1)} fusion(bf16[128,64,1024]{2,1,0:T(8,128)(2,1)} %param.10, s32[1024]{0:T(1024)S(1)} %pad_clamp_fusion), kind=kCustom, calls=%fused_computation.3 | custom fusion | bytes 2097184 | tf_op jit(solution)/shard_map/gather | solution.py:32
  19.1 1.1 broadcast_select_fusion
  20.2 3.6 %all-to-all-start.1 = ((bf16[2,4,64,1024]{3,2,1,0:T(8,128)(2,1)}), bf16[2,4,64,1024]{3,2,1,0:T(8,128)(2,1)S(1)}, u32[]{:S(2)}, u32[]{:S(2)}) async-start(bf16[2,4,64,1024]{3,2,1,0:T(8,128)(2,1)} %broadcast_select_fusion), calls=%async_computation.1 | async-start | bytes 2097152 | tf_op jit(solution)/shard_map/all_to_all | solution.py:37
  23.9 0.6 gather_fusion
  24.6 1.3 all-to-all-done.1
  25.9 1.2 select_reduce_fusion
  27.1 6.4 %gather_fusion.2 = bf16[8,1024,64]{1,2,0:T(8,128)(2,1)S(1)} fusion(bf16[128,1024,64]{1,2,0:T(8,128)(2,1)} %param.9, s32[1024]{0:T(1024)S(1)} %pad_clamp_fusion), kind=kCustom, calls=%fused_computation.2 | custom fusion | bytes 2097184 | tf_op jit(solution)/shard_map/gather | solution.py:30
  33.5 1.1 broadcast_select_fusion.1
  34.6 3.6 %all-to-all-start = ((bf16[2,4,1024,64]{2,3,1,0:T(8,128)(2,1)}), bf16[2,4,1024,64]{2,3,1,0:T(8,128)(2,1)S(1)}, u32[]{:S(2)}, u32[]{:S(2)}) async-start(bf16[2,4,1024,64]{2,3,1,0:T(8,128)(2,1)} %broadcast_select_fusion.1), calls=%async_computation | async-start | bytes 2097152 | tf_op jit(solution)/shard_map/all_to_all | solution.py:36
  38.2 0.0 reduce-scatter.2.cloned.1.call-start
  38.3 0.1 reshape.119
  38.4 1.9 %all-to-all-done = bf16[2,4,1024,64]{2,3,1,0:T(8,128)(2,1)S(1)} async-done(((bf16[2,4,1024,64]{2,3,1,0:T(8,128)(2,1)}), bf16[2,4,1024,64]{2,3,1,0:T(8,128)(2,1)S(1)}, u32[]{:S(2)}, u32[]{:S(2)}) %all-to-all-start) | async-done | bytes 1048608 | tf_op jit(solution)/shard_map/all_to_all | solution.py:36
  40.3 0.4 select_reduce_fusion.1
  40.7 0.2 convolution_multiply_fusion
  41.0 62.2 %all-gather.2.cloned.1.call-done = bf16[4,64,8192]{2,1,0:T(8,128)(2,1)} async-done(((bf16[4,64,1024]{2,1,0:T(8,128)(2,1)}), bf16[4,64,8192]{2,1,0:T(8,128)(2,1)}) %all-gather.2.cloned.1.call-update) | async-done | bytes 4194320 | tf_op jit(solution)/shard_map/all_gather | solution.py:51
  103.2 3.5 %fusion.3 = f32[4,16,8192]{2,1,0:T(8,128)S(1)} fusion(f32[4,64,16]{1,2,0:T(8,128)S(1)} %convolution_multiply_fusion, bf16[4,64,8192]{2,1,0:T(8,128)(2,1)} %all-gather.2.cloned.1.call-done), kind=kOutput, calls=%fused_computation.32 | convolution fusion | flops 402653184 | bytes 6307840 | tf_op jit(solution)/shard_map/bkr,brc->bkc/dot_general | solution.py:54
  106.7 10.2 %convolution_add_fusion = f32[64,8192]{1,0:T(8,128)} fusion(f32[64,8192]{1,0:T(8,128)S(1)} %bitcast.16, bf16[64,1024]{1,0:T(8,128)(2,1)S(1)} %copy-done, bf16[1024,8192]{1,0:T(8,128)(2,1)} %param.8), kind=kOutput, calls=%fused_computation.4 | convolution fusion | flops 1074266112 | bytes 21102592 | tf_op jit(solution)/shard_map/dot_general | solution.py:53
  116.9 66.7 %reduce-scatter.2.cloned.1.call-done = f32[64,1024]{1,0:T(8,128)} async-done(((f32[64,8192]{1,0:T(8,128)}), f32[64,1024]{1,0:T(8,128)}) %reduce-scatter.2.cloned.1.call-update) | async-done | bytes 262160 | tf_op jit(solution)/shard_map/reduce_scatter | solution.py:58
  183.7 1.6 convert_element_type.2
  (22 shorter events, 0.2 us)
Async XLA Ops:
  6.5 34.2 %copy-start = (bf16[64,1024]{1,0:T(8,128)(2,1)S(1)}, bf16[64,1024]{1,0:T(8,128)(2,1)}, u32[]{:S(2)}) copy-start(bf16[64,1024]{1,0:T(8,128)(2,1)} %param.7) | copy-start | bytes 393220
  6.5 17.3 %copy-start.2 = (s32[4]{0:T(128)S(1)}, s32[4]{0:T(128)}, u32[]{:S(2)}) copy-start(s32[4]{0:T(128)} %param.12) | copy-start | bytes 52
  6.5 17.4 %copy-start.1 = (s32[256]{0:T(256)S(1)}, s32[256]{0:T(256)}, u32[]{:S(2)}) copy-start(s32[256]{0:T(256)} %param.11) | copy-start | bytes 3076
  20.2 5.7 %all-to-all-start.1 = ((bf16[2,4,64,1024]{3,2,1,0:T(8,128)(2,1)}), bf16[2,4,64,1024]{3,2,1,0:T(8,128)(2,1)S(1)}, u32[]{:S(2)}, u32[]{:S(2)}) async-start(bf16[2,4,64,1024]{3,2,1,0:T(8,128)(2,1)} %broadcast_select_fusion), calls=%async_computation.1 | async-start | bytes 2097152 | tf_op jit(solution)/shard_map/all_to_all | solution.py:37
  23.8 79.4 %all-gather.2.cloned.1.call-start = ((), (), s32[]{:S(2)}) async-start(), calls=%async_computation.3 | async-start | bytes 4718592 | tf_op jit(solution)/shard_map/all_gather | solution.py:51
  27.1 11.2 %copy-start.3 = (s32[64]{0:T(128)S(1)}, s32[64]{0:T(128)}, u32[]{:S(2)}) copy-start(s32[64]{0:T(128)} %param.13) | copy-start | bytes 772
  34.6 5.7 %all-to-all-start = ((bf16[2,4,1024,64]{2,3,1,0:T(8,128)(2,1)}), bf16[2,4,1024,64]{2,3,1,0:T(8,128)(2,1)S(1)}, u32[]{:S(2)}, u32[]{:S(2)}) async-start(bf16[2,4,1024,64]{2,3,1,0:T(8,128)(2,1)} %broadcast_select_fusion.1), calls=%async_computation | async-start | bytes 2097152 | tf_op jit(solution)/shard_map/all_to_all | solution.py:36
  38.2 145.4 %reduce-scatter.2.cloned.1.call-start = ((), (), s32[]{:S(2)}) async-start(), calls=%async_computation.4 | async-start | bytes 2359296 | tf_op jit(solution)/shard_map/reduce_scatter | solution.py:58
Sparse Core Ops, SparseCore 0:
  27.2 75.9 all-gather.1
  117.0 66.5 reduce-scatter.1
where the time goes:
time: 193 us; the launch traced here: 192 us
  waiting for transfers between devices  132 us (68%)
  local copies, waits for them, and re-layouts  17 us (9%)
  between operations  14.2 us (7%)
  matrix products  13.9 us (7%)
  starting transfers between devices  7.27 us (4%)
  other arithmetic  5.48 us (3%)
    reduce_scatter x1, waiting for transfers between devices, shards(): lax.psum_scatter(partial_value, 'tensor', scatter_dimension=1, tiled=True)  66.7 us
    all_gather x1, waiting for transfers between devices, shards(): piece = lax.all_gather(fetched_up, 'tensor', axis=2, tiled=True)  62.2 us
    dot_general x1, matrix products, shards(): jnp.dot(acts, base_output_matrix, preferred_element_type=jnp.float32)  10.2 us
    gather x1, local copies, waits for them, and re-layouts, shards(): stored_down_factors[local_row_index]  6.39 us
    gather x1, local copies, waits for them, and re-layouts, shards(): stored_up_factors[local_row_index]  6.38 us
  transfers between devices with their start and end apart: 4, of which 4 were waited for; matrix products, arithmetic and copies ran while one was open for 5% of the time, Pallas kernels for 0%

commit v1 on v0

v1 whole, which is shorter than its diff:
```python
import jax
import jax.numpy as jnp
from jax import lax
from jax.sharding import PartitionSpec as P


def shards(
    acts,
    base_output_matrix,
    stored_down_factors,
    stored_up_factors,
    adapter_storage_row,
    adapter_per_block,
    adapter_per_token,
):
    tok_rows, feature_list = acts.shape
    owned = stored_down_factors.shape[0]
    block_count = adapter_per_block.shape[0]
    block_rows = tok_rows // block_count
    wanted = lax.all_gather(adapter_per_block, "replica", axis=0, tiled=True)
    every = lax.all_gather(acts, "replica", axis=0, tiled=True)
    blocks = wanted.shape[0]
    stored = adapter_storage_row[wanted]
    here = (stored // owned == lax.axis_index("replica")).astype(jnp.float32)[:, None, None]
    local = stored % owned
    shrunk_part = jnp.einsum(
        "bkf,bfr->bkr",
        every.reshape(blocks, block_rows, feature_list),
        stored_down_factors[local],
        preferred_element_type=jnp.float32,
    )
    shrunk = lax.psum(shrunk_part * here, "tensor")
    delta_all = jnp.einsum(
        "bkr,brc->bkc",
        shrunk,
        stored_up_factors[local].astype(jnp.float32),
        precision=lax.Precision.HIGHEST,
    )
    delta = lax.psum_scatter(
        delta_all.reshape(blocks * block_rows, -1), "replica", scatter_dimension=0, tiled=True
    )
    part_base = jnp.dot(acts, base_output_matrix, preferred_element_type=jnp.float32)
    base = lax.psum_scatter(part_base, "tensor", scatter_dimension=1, tiled=True)
    alive = (adapter_per_token >= 0)[:, None]
    return (base + jnp.where(alive, delta, 0.0)).astype(jnp.bfloat16)


def solution(mesh):
    placed = (
        P(("groups", "replica"), "tensor"),
        P("tensor", None),
        P("replica", "tensor", None),
        P("replica", None, "tensor"),
        P(),
        P(("groups", "replica")),
        P(("groups", "replica")),
    )
    return jax.shard_map(
        shards,
        mesh=mesh,
        in_specs=placed,
        out_specs=P(("groups", "replica"), "tensor"),
        check_vma=False,
    )
```

time: 193 us -> 155 us (0.80)
  waiting for transfers between devices: 132 us -> 67.6 us
  blocking collectives: 1.92 us -> 43.3 us
  starting transfers between devices: 7.27 us -> 0.04 us
  other arithmetic: 5.48 us -> 1.83 us
    all_gather x1 -> x0, waiting for transfers between devices: 62.2 us -> none  [shards(): piece = lax.all_gather(fetched_up, 'tensor', axis=2, tiled=True)]
    psum x0 -> x1, blocking collectives: none -> 39.2 us  [shards(): shrunk = lax.psum(shrunk_part * here, 'tensor')]
    all_to_all x2 -> x0, starting transfers between devices: 7.19 us -> none  [the longest x1 3.61 us: shards(): lax.all_to_all(outgoing_down, 'replica', split_axis=0, concat_axis=0, til...]
    all_to_all x2 -> x0, waiting for transfers between devices: 3.29 us -> none  [the longest x1 1.95 us: shards(): lax.all_to_all(outgoing_down, 'replica', split_axis=0, concat_axis=0, til...]
    select_n x5 -> x1, other arithmetic: 2.26 us -> 0.01 us  [shards(): stored_down_factors[local]]
    all_gather x0 -> x1, blocking collectives: none -> 2.21 us  [shards(): every = lax.all_gather(acts, 'replica', axis=0, tiled=True)]
    dot_general x2, matrix products: 3.75 us -> 1.71 us  [the longest x1 1.33 us: shards(): jnp.einsum('bkr,brc->bkc', shrunk, stored_up_factors[local].astype(jnp.fl...]
    reduce_scatter x1 -> x2, waiting for transfers between devices: 66.7 us -> 67.6 us  [the longest x1 67.6 us: shards(): lax.psum_scatter(part_base, 'tensor', scatter_dimension=1, tiled=True)]
  transfers between devices with their start and end apart: 4 -> 2, of which waited for: 4 -> 1; matrix products, arithmetic and copies ran while one was open for 5% -> 7% of each run, Pallas kernels for 0% -> 0%
where the time goes in v1:
time: 155 us
  waiting for transfers between devices  67.6 us (44%)
  blocking collectives  43.3 us (28%)
  local copies, waits for them, and re-layouts  15.5 us (10%)
  between operations  14.1 us (9%)
  matrix products  12.2 us (8%)
  other arithmetic  1.83 us (1%)
    reduce_scatter x1, waiting for transfers between devices, shards(): lax.psum_scatter(part_base, 'tensor', scatter_dimension=1, tiled=True)  67.6 us
    psum x1, blocking collectives, shards(): shrunk = lax.psum(shrunk_part * here, 'tensor')  39.2 us
    dot_general x1, matrix products, shards(): jnp.dot(acts, base_output_matrix, preferred_element_type=jnp.float32)  10.5 us
    gather x1, local copies, waits for them, and re-layouts, shards(): stored_down_factors[local]  6.39 us
    gather x1, local copies, waits for them, and re-layouts, shards(): stored_up_factors[local].astype(jnp.float32)  6.38 us
  transfers between devices with their start and end apart: 2, of which 1 were waited for; matrix products, arithmetic and copies ran while one was open for 7% of the time, Pallas kernels for 0%

profile of v1, /device:TPU:0, one launch (start us, length us, event | category | flops | bytes accessed | tf_op | source)
XLA Modules:
  0.0 154.6 jit_solution(1989873322626736395)
XLA Ops:
  6.5 0.0 copy-start
  6.5 0.0 reduce-scatter.5.cloned.1.call-start
  6.5 1.2 dynamic-slice
  8.4 0.9 dynamic-update-slice
  9.3 1.9 %all-reduce = s32[8]{0:T(128)S(1)} all-reduce(s32[8]{0:T(128)S(1)} %dynamic-update-slice), channel_id=1, replica_groups=mesh['groups'=2,'replica'=2,'tensor'=8] {'replica'}, use_global_device_ids=true, to_apply=%add | all-reduce | flops 8 | bytes 64
  11.2 0.0 copy-done
  11.3 0.6 gather_fusion
  11.9 2.2 %all_gather.7 = bf16[128,1024]{1,0:T(8,128)(2,1)S(1)} all-gather(bf16[64,1024]{1,0:T(8,128)(2,1)} %param.7), channel_id=1, replica_groups=mesh['groups'=2,'replica'=2,'tensor'=8] {'replica'}, dimensions={0}, use_global_device_ids=true | all-gather | bytes 393216 | tf_op jit(solution)/shard_map/all_gather | solution.py:21
  14.1 0.0 copy-start.1
  14.2 6.4 %gather_fusion.1 = bf16[8,1024,64]{1,2,0:T(8,128)(2,1)S(1)} fusion(bf16[128,1024,64]{1,2,0:T(8,128)(2,1)} %param.9, s32[1024]{0:T(1024)S(1)} %pad_clamp_fusion), kind=kCustom, calls=%fused_computation.1 | custom fusion | bytes 2097184 | tf_op jit(solution)/shard_map/gather | solution.py:29
  20.6 0.4 fusion
  20.9 39.2 %psum.7 = f32[8,16,64]{2,1,0:T(8,128)S(1)} all-reduce(f32[8,16,64]{2,1,0:T(8,128)S(1)} %fusion), channel_id=1, replica_groups=mesh['groups'=2,'replica'=2,'tensor'=8] {'tensor'}, use_global_device_ids=true, to_apply=%region_1.2 | all-reduce | flops 8192 | bytes 65536 | tf_op jit(solution)/shard_map/psum | solution.py:32
  60.1 6.4 %gather_fusion.2 = bf16[8,64,1024]{2,1,0:T(8,128)(2,1)S(1)} fusion(bf16[128,64,1024]{2,1,0:T(8,128)(2,1)} %param.10, s32[1024]{0:T(1024)S(1)} %pad_clamp_fusion), kind=kCustom, calls=%fused_computation.2 | custom fusion | bytes 2097184 | tf_op jit(solution)/shard_map/gather | solution.py:36
  66.5 1.3 fusion.4
  67.8 0.0 reduce-scatter.5.cloned.1.call-update
  67.8 0.0 reduce-scatter.3.cloned.1.call-start
  67.9 10.5 %fusion.3 = f32[64,8192]{1,0:T(8,128)} fusion(bf16[64,1024]{1,0:T(8,128)(2,1)} %param.7, bf16[1024,8192]{1,0:T(8,128)(2,1)} %param.8), kind=kOutput, calls=%fused_computation.21 | convolution fusion | flops 1073741824 | bytes 19005440 | tf_op jit(solution)/shard_map/dot_general | solution.py:42
  78.4 0.0 reduce-scatter.3.cloned.1.call-update
  78.4 0.0 copy-done.1
  78.4 0.0 reduce-scatter.5.cloned.1.call-done
  78.5 67.6 %reduce-scatter.3.cloned.1.call-done = f32[64,1024]{1,0:T(8,128)} async-done(((f32[64,8192]{1,0:T(8,128)}), f32[64,1024]{1,0:T(8,128)}) %reduce-scatter.3.cloned.1.call-update) | async-done | bytes 262160 | tf_op jit(solution)/shard_map/reduce_scatter | solution.py:43
  146.0 1.8 %add_convert_fusion = bf16[64,1024]{1,0:T(8,128)(2,1)} fusion(f32[64,1024]{1,0:T(8,128)} %reduce-scatter.3.cloned.1.call-done, f32[64,1024]{1,0:T(8,128)} %reduce-scatter.5.cloned.1.call-done, pred[64]{0:T(512)(128)(4,1)S(1)} %broadcast_compare_fusion), kind=kLoop, calls=%fused_computation.5 | loop fusion | flops 196608 | bytes 655424 | tf_op jit(solution)/shard_map/convert_element_type | solution.py:45
  (7 shorter events, 0.1 us)
Async XLA Ops:
  6.5 4.7 %copy-start = (s32[256]{0:T(256)S(1)}, s32[256]{0:T(256)}, u32[]{:S(2)}) copy-start(s32[256]{0:T(256)} %param.11) | copy-start | bytes 3076
  6.5 71.9 %reduce-scatter.5.cloned.1.call-start = ((), (), s32[]{:S(2)}) async-start(), calls=%async_computation.3 | async-start | bytes 786432 | tf_op jit(solution)/shard_map/reduce_scatter | solution.py:39
  14.1 64.3 %copy-start.1 = (s32[64]{0:T(128)S(1)}, s32[64]{0:T(128)}, u32[]{:S(2)}) copy-start(s32[64]{0:T(128)} %param.13) | copy-start | bytes 772
  67.8 78.2 %reduce-scatter.3.cloned.1.call-start = ((), (), s32[]{:S(2)}) async-start(), calls=%async_computation.2 | async-start | bytes 2359296 | tf_op jit(solution)/shard_map/reduce_scatter | solution.py:43
Sparse Core Ops, SparseCore 0:
  68.0 5.2 reduce-scatter.4
  78.5 67.4 reduce-scatter.2

commit v2 on v1

--- a/solution.py
+++ b/solution.py
@@ -1,7 +1,241 @@
+import functools
+
 import jax
 import jax.numpy as jnp
 from jax import lax
+from jax.experimental import pallas as pl
+from jax.experimental.pallas import tpu as pltpu
 from jax.sharding import PartitionSpec as P
+
+MESH = pl.DeviceIdType.MESH
+F32 = jnp.float32
+TAIL = 128
+LEVELS = 32000.0
+HOPS = (2, 1, 3, 0)
+
+
+def pick_kernel(owned, wanted, table, acts, others, mask, down, up, shrunk, chosen, rows, down_sem, up_sem):
+    me = lax.axis_index("replica")
+    count = wanted.shape[0]
+    half = count // 2
+    stored = [table[wanted[b]] for b in range(count)]
+    copies = []
+    for b in range(count):
+        spot = lax.rem(stored[b], owned)
+        first = pltpu.make_async_copy(down.at[spot], rows.at[b], down_sem.at[b])
+        second = pltpu.make_async_copy(up.at[spot], chosen.at[b], up_sem.at[b])
+        copies.append((first, second))
+    for first, _ in copies:
+        first.start()
+    for _, second in copies:
+        second.start()
+    step = acts.shape[0] // half
+    sides = []
+    for side, source in ((0, acts), (1, others)):
+        parts = []
+        for b in range(half):
+            at = side * half + b
+            copies[at][0].wait()
+            part = lax.dot_general(
+                source[b * step : (b + 1) * step, :],
+                rows[at],
+                (((1,), (1,)), ((), ())),
+                preferred_element_type=F32,
+            )
+            parts.append(part * (lax.div(stored[at], owned) == me).astype(F32))
+        sides.append(jnp.concatenate(parts, axis=0))
+    shrunk[...] = jnp.concatenate(sides, axis=1) * mask[...]
+    for _, second in copies:
+        second.wait()
+
+
+def encode(value, slot):
+    width = value.shape[1]
+    largest = jnp.maximum(jnp.max(jnp.abs(value), axis=1, keepdims=True), 1e-30)
+    level = jnp.ceil(jnp.log2(largest))
+    factor = jnp.exp2(-level) * LEVELS
+    coded = jnp.round(jnp.clip(value * factor, -32767.0, 32767.0))
+    slot[:, 0:width] = coded.astype(jnp.int32).astype(jnp.int16)
+    slot[:, width : width + TAIL] = (
+        jnp.broadcast_to(level, (value.shape[0], TAIL)).astype(jnp.int32).astype(jnp.int16)
+    )
+
+
+def decode(slot, width):
+    level = slot[:, width : width + TAIL].astype(jnp.int32).astype(F32)[:, 0:1]
+    return slot[:, 0:width].astype(jnp.int32).astype(F32) * (jnp.exp2(level) * (1.0 / LEVELS))
+
+
+def main_kernel(
+    acts, matrix, shrunk, chosen, out,
+    weights, x_out, x_in, z_out, z_in, s_pair, s_sum, s_in, total, d_out, d_in,
+    w_sem, x_send, x_recv, z_send, z_recv, s_send, s_recv, d_send, d_recv,
+):
+    g = lax.axis_index("groups")
+    r = lax.axis_index("replica")
+    t = lax.axis_index("tensor")
+    z, x = lax.div(t, 2), lax.rem(t, 2)
+    width = out.shape[1]
+    far = [lax.rem(z + k, 4) for k in HOPS]
+    pair = (g, r, 2 * z + (1 - x))
+    peers = [(g, r, 2 * far[i] + x) for i in range(3)]
+    twin = (g, 1 - r, t)
+
+    loads = []
+    for i in range(4):
+        for j, column in enumerate((1 - x, x)):
+            place = pl.multiple_of((2 * far[i] + column) * width, width)
+            loads.append(
+                pltpu.make_async_copy(
+                    matrix.at[:, pl.ds(place, width)], weights.at[2 * i + j], w_sem.at[2 * i + j]
+                )
+            )
+    for load in loads:
+        load.start()
+
+    barrier = pltpu.get_barrier_semaphore()
+    for device in [pair, twin] + peers:
+        pl.semaphore_signal(barrier, inc=1, device_id=device, device_id_type=MESH)
+    pl.semaphore_wait(barrier, 5)
+
+    def send(source, target, one, two, device):
+        copy = pltpu.make_async_remote_copy(
+            src_ref=source, dst_ref=target, send_sem=one, recv_sem=two,
+            device_id=device, device_id_type=MESH,
+        )
+        copy.start()
+        return copy
+
+    def product(at):
+        loads[at].wait()
+        return jnp.dot(acts[...], weights[at], preferred_element_type=F32)
+
+    s_copies = [send(shrunk, s_pair, s_send.at[3], s_recv.at[3], pair)]
+    x_copies = []
+    z_copies = []
+
+    def x_step(i):
+        encode(product(2 * i), x_out.at[i])
+        x_copies.append(send(x_out.at[i], x_in.at[i], x_send.at[i], x_recv.at[i], pair))
+
+    x_step(0)
+    x_step(1)
+    s_copies[0].wait_recv()
+    s_sum[...] = shrunk[...] + s_pair[...]
+    for i in range(3):
+        s_copies.append(send(s_sum, s_in.at[i], s_send.at[i], s_recv.at[i], peers[i]))
+    for i in range(3):
+        if i < 2:
+            x_step(i + 2)
+        mine = product(2 * i + 1)
+        x_copies[i].wait_recv()
+        encode(mine + decode(x_in.at[i], width), z_out.at[i])
+        z_copies.append(send(z_out.at[i], z_in.at[i], z_send.at[i], z_recv.at[i], peers[i]))
+    total[...] = product(7)
+
+    for copy in s_copies[1:]:
+        copy.wait_recv()
+    full = s_sum[...] + s_in[0] + s_in[1] + s_in[2]
+    high = full.astype(jnp.bfloat16)
+    rest = full - high.astype(F32)
+    middle = rest.astype(jnp.bfloat16)
+    low = (rest - middle.astype(F32)).astype(jnp.bfloat16)
+    half = chosen.shape[0] // 2
+    rank = chosen.shape[1]
+    step = acts.shape[0] // half
+
+    def delta(side, b):
+        rows = slice(b * step, (b + 1) * step)
+        lanes = slice(side * rank, (side + 1) * rank)
+        three = jnp.concatenate([high[rows, lanes], middle[rows, lanes], low[rows, lanes]], axis=0)
+        got = jnp.dot(three, chosen[side * half + b], preferred_element_type=F32)
+        return got[0:step] + got[step : 2 * step] + got[2 * step : 3 * step]
+
+    for b in range(half):
+        d_out[b * step : (b + 1) * step, :] = delta(1, b)
+    d_copy = send(d_out, d_in, d_send, d_recv, twin)
+    for b in range(half):
+        total[b * step : (b + 1) * step, :] += delta(0, b)
+    d_copy.wait_recv()
+    total[...] += d_in[...]
+    x_copies[3].wait_recv()
+    total[...] += decode(x_in.at[3], width)
+    for i in range(2):
+        z_copies[i].wait_recv()
+        total[...] += decode(z_in.at[i], width)
+    z_copies[2].wait_recv()
+    out[...] = (total[...] + decode(z_in.at[2], width)).astype(out.dtype)
+    for copy in s_copies + x_copies + z_copies + [d_copy]:
+        copy.wait_send()
+
+
+def kernel_shards(
+    acts,
+    base_output_matrix,
+    stored_down_factors,
+    stored_up_factors,
+    adapter_storage_row,
+    adapter_per_block,
+    adapter_per_token,
+):
+    rows, features = acts.shape
+    owned, _, rank = stored_down_factors.shape
+    width = stored_up_factors.shape[2]
+    half = adapter_per_block.shape[0]
+    names = jnp.concatenate([adapter_per_block, adapter_per_token])
+    other_names = lax.ppermute(names, "replica", [(0, 1), (1, 0)])
+    others = lax.ppermute(acts, "replica", [(0, 1), (1, 0)])
+    wanted = jnp.concatenate([adapter_per_block, other_names[:half]])
+    both = jnp.stack([adapter_per_token, other_names[half:]], axis=1)
+    mask = jnp.repeat((both >= 0).astype(F32), rank, axis=1)
+    smem = pl.BlockSpec(memory_space=pltpu.SMEM)
+    vmem = pl.BlockSpec(memory_space=pltpu.VMEM)
+    anywhere = pl.BlockSpec(memory_space=pl.ANY)
+    shrunk, chosen = pl.pallas_call(
+        functools.partial(pick_kernel, owned),
+        out_shape=[
+            jax.ShapeDtypeStruct((rows, 2 * rank), F32),
+            jax.ShapeDtypeStruct((2 * half, rank, width), jnp.bfloat16),
+        ],
+        in_specs=[smem, smem, vmem, vmem, vmem, anywhere, anywhere],
+        out_specs=[vmem, vmem],
+        scratch_shapes=[
+            pltpu.VMEM((2 * half, rank, features), jnp.bfloat16),
+            pltpu.SemaphoreType.DMA((2 * half,)),
+            pltpu.SemaphoreType.DMA((2 * half,)),
+        ],
+        compiler_params=pltpu.CompilerParams(vmem_limit_bytes=16 * 2**20),
+        name="pick",
+    )(
+        wanted, adapter_storage_row, acts, others, mask,
+        jnp.swapaxes(stored_down_factors, 1, 2), stored_up_factors,
+    )
+    coded = (rows, width + TAIL)
+    dma = pltpu.SemaphoreType.DMA
+    return pl.pallas_call(
+        main_kernel,
+        out_shape=jax.ShapeDtypeStruct((rows, width), jnp.bfloat16),
+        in_specs=[vmem, anywhere, vmem, vmem],
+        out_specs=vmem,
+        scratch_shapes=[
+            pltpu.VMEM((8, features, width), jnp.bfloat16),
+            pltpu.VMEM((4,) + coded, jnp.int16),
+            pltpu.VMEM((4,) + coded, jnp.int16),
+            pltpu.VMEM((3,) + coded, jnp.int16),
+            pltpu.VMEM((3,) + coded, jnp.int16),
+            pltpu.VMEM((rows, 2 * rank), F32),
+            pltpu.VMEM((rows, 2 * rank), F32),
+            pltpu.VMEM((3, rows, 2 * rank), F32),
+            pltpu.VMEM((rows, width), F32),
+            pltpu.VMEM((rows, width), F32),
+            pltpu.VMEM((rows, width), F32),
+            dma((8,)), dma((4,)), dma((4,)), dma((3,)), dma((3,)), dma((4,)), dma((4,)), dma, dma,
+        ],
+        compiler_params=pltpu.CompilerParams(
+            collective_id=0, has_side_effects=True, vmem_limit_bytes=40 * 2**20
+        ),
+        name="main",
+    )(acts, base_output_matrix, shrunk, chosen)
 
 
 def shards(
@@ -55,8 +289,9 @@
         P(("groups", "replica")),
         P(("groups", "replica")),
     )
+    fits = mesh.shape["tensor"] == 8 and mesh.shape["replica"] == 2
     return jax.shard_map(
-        shards,
+        kernel_shards if fits else shards,
         mesh=mesh,
         in_specs=placed,
         out_specs=P(("groups", "replica"), "tensor"),

time: 155 us -> 49.3 us (0.32)
  waiting for transfers between devices: 67.6 us -> 0.76 us
  blocking collectives: 43.3 us -> 0 us
  Pallas kernels: 0 us -> 31.4 us
  between operations: 14.1 us -> 0.04 us
  matrix products: 12.2 us -> 0 us
    reduce_scatter x2 -> x0, waiting for transfers between devices: 67.6 us -> none  [the longest x1 67.6 us: shards(): lax.psum_scatter(part_base, 'tensor', scatter_dimension=1, tiled=True)]
    psum x1 -> x0, blocking collectives: 39.2 us -> none  [shards(): shrunk = lax.psum(shrunk_part * here, 'tensor')]
    pallas_call x0 -> x2, Pallas kernels: none -> 31.4 us  [the longest x1 26.4 us: kernel_shards(): pl.pallas_call(main_kernel, out_shape=jax.ShapeDtypeStruct((rows, width),...]
    gather x3 -> x0, local copies, waits for them, and re-layouts: 13.4 us -> none  [the longest x1 6.39 us: shards(): stored_down_factors[local]]
    dot_general x3 -> x0, matrix products: 12.2 us -> none  [the longest x1 10.5 us: shards(): jnp.dot(acts, base_output_matrix, preferred_element_type=jnp.float32)]
    unnamed x7 -> x11, local copies, waits for them, and re-layouts: 2.12 us -> 13.8 us
    all_gather x1 -> x0, blocking collectives: 2.21 us -> none  [shards(): every = lax.all_gather(acts, 'replica', axis=0, tiled=True)]
    unnamed x1 -> x0, blocking collectives: 1.92 us -> none
  transfers between devices with their start and end apart: 2 -> 2, of which waited for: 1 -> 1; matrix products, arithmetic and copies ran while one was open for 7% -> 4% of each run, Pallas kernels for 0% -> 0%
where the time goes in v2:
time: 49.3 us; the launch traced here: 49.1 us
  Pallas kernels  31.4 us (64%)
  local copies, waits for them, and re-layouts  14.2 us (29%)
  other arithmetic  2.14 us (4%)
  waiting for transfers between devices  0.76 us (2%)
  starting transfers between devices  0.52 us (1%)
    pallas_call x1, Pallas kernels, kernel_shards(): pl.pallas_call(main_kernel, out_shape=jax.ShapeDtypeStruct((rows, width),...  26.4 us
    unnamed x11, local copies, waits for them, and re-layouts  13.8 us
    pallas_call x1, Pallas kernels, kernel_shards(): pl.pallas_call(functools.partial(pick_kernel, owned), out_shape=[jax.Shap...  4.99 us
  transfers between devices with their start and end apart: 2, of which 1 were waited for; matrix products, arithmetic and copies ran while one was open for 4% of the time, Pallas kernels for 0%

profile of v2, /device:TPU:0, one launch (start us, length us, event | category | flops | bytes accessed | tf_op | source)
XLA Modules:
  0.0 49.1 jit_solution(7858897222344083215)
XLA Ops:
  0.0 0.7 %pad_add_fusion = s32[68]{0:T(128)S(1)} fusion(s32[64]{0:T(128)} %param.13, s32[4]{0:T(128)} %param.12), kind=kLoop, calls=%fused_computation.1 | loop fusion | flops 68 | bytes 544 | tf_op jit(solution)/shard_map/concatenate | solution.py:185
  0.7 0.5 collective-permute-start
  1.2 0.1 collective-permute-start.1
  1.3 0.8 %collective-permute-done = s32[68]{0:T(128)S(1)} collective-permute-done((s32[68]{0:T(128)S(1)}, s32[68]{0:T(128)S(1)}, u32[]{:S(2)}, u32[]{:S(2)}) %collective-permute-start) | collective-permute-done | bytes 304 | tf_op jit(solution)/shard_map/ppermute | solution.py:186
  2.0 0.1 slice_bitcast_fusion
  2.1 0.7 %compare_convert_fusion = f32[64,2]{0,1:T(2,128)S(1)} fusion(s32[64,1]{0,1:T(1,128)S(1)} %slice_bitcast_fusion, s32[64,1]{0,1:T(1,128)} %bitcast.6), kind=kLoop, calls=%fused_computation | loop fusion | flops 384 | bytes 1024 | tf_op jit(solution)/shard_map/convert_element_type | solution.py:190
  2.8 0.1 copy.8
  2.9 0.1 broadcast_in_dim.3
  3.0 0.1 reshape.3.mask
  3.1 0.7 %pad_add_fusion.1.wanted = s32[8]{0:T(128)S(1)} fusion(s32[4]{0:T(128)S(1)} %bitcast.7, s32[4]{0:T(128)} %param.12), kind=kLoop, calls=%fused_computation.2 | loop fusion | flops 8 | bytes 64 | tf_op jit(solution)/shard_map/concatenate | solution.py:188
  3.8 0.0 collective-permute-done.1.others
  3.8 0.0 copy-start
  3.8 5.8 %copy-done = bf16[128,1024,64]{1,2,0:T(8,128)(2,1)S(1)} copy-done((bf16[128,1024,64]{1,2,0:T(8,128)(2,1)S(1)}, bf16[128,1024,64]{1,2,0:T(8,128)(2,1)}, u32[]{:S(2)}) %copy-start) | copy-done | bytes 16777240
  9.6 0.0 copy-start.1
  9.6 5.8 %copy-done.1 = bf16[128,64,1024]{2,1,0:T(8,128)(2,1)S(1)} copy-done((bf16[128,64,1024]{2,1,0:T(8,128)(2,1)S(1)}, bf16[128,64,1024]{2,1,0:T(8,128)(2,1)}, u32[]{:S(2)}) %copy-start.1) | copy-done | bytes 16777240
  15.4 0.0 copy-start.2
  15.4 0.9 %copy-done.2 = bf16[64,1024]{1,0:T(8,128)(2,1)S(1)} copy-done((bf16[64,1024]{1,0:T(8,128)(2,1)S(1)}, bf16[64,1024]{1,0:T(8,128)(2,1)}, u32[]{:S(2)}) %copy-start.2) | copy-done | bytes 131096
  16.3 0.0 copy-start.4
  16.3 0.7 %copy-done.4 = s32[256]{0:T(256)S(1)} copy-done((s32[256]{0:T(256)S(1)}, s32[256]{0:T(256)}, u32[]{:S(2)}) %copy-start.4) | copy-done | bytes 1048
  16.9 0.0 copy-start.3
  17.0 5.0 %pick.1 = (f32[64,128]{1,0:T(8,128)S(1)}, bf16[8,64,1024]{2,1,0:T(8,128)(2,1)S(1)}) custom-call(s32[8]{0:T(128)S(1)} %pad_add_fusion.1.wanted, s32[256]{0:T(256)S(1)} %copy-done.4, bf16[64,1024]{1,0:T(8,128)(2,1)S(1)} %copy-done.2, bf16[64,1024]{1,0:T(8,128)(2,1)S(1)} %collective-permute-done.1.others, f32[64,128]{1,0:T(8,128)S(1)} %reshape.3.mask, ...), custom_call_target="tpu_custom_call" | custom-call | tf_op jit(solution)/shard_map/pick/pallas_call | solution.py:194
  22.0 0.0 copy-done.3
  22.0 26.4 %main.1 = bf16[64,1024]{1,0:T(8,128)(2,1)S(1)} custom-call(bf16[64,1024]{1,0:T(8,128)(2,1)S(1)} %copy-done.3, bf16[1024,8192]{1,0:T(8,128)(2,1)} %matrix.1, f32[64,128]{1,0:T(8,128)S(1)} %get-tuple-element.7.shrunk, bf16[8,64,1024]{2,1,0:T(8,128)(2,1)S(1)} %get-tuple-element.8.chosen), custom_call_target="tpu_custom_call" | custom-call | tf_op jit(solution)/shard_map/main/pallas_call | solution.py:215
  48.4 0.7 %copy.10 = bf16[64,1024]{1,0:T(8,128)(2,1)} copy(bf16[64,1024]{1,0:T(8,128)(2,1)S(1)} %main.1) | data formatting | bytes 262144
Async XLA Ops:
  0.7 1.3 %collective-permute-start = (s32[68]{0:T(128)S(1)}, s32[68]{0:T(128)S(1)}, u32[]{:S(2)}, u32[]{:S(2)}) collective-permute-start(s32[68]{0:T(128)S(1)} %pad_add_fusion), channel_id=1, source_target_pairs={{0,8},{8,0},{1,9},{9,1},{2,10},{10,2},{3,11},{11,3},{4,12},{12,4},... | collective-permute-start | bytes 824 | tf_op jit(solution)/shard_map/ppermute | solution.py:186
  1.2 2.6 %collective-permute-start.1 = (bf16[64,1024]{1,0:T(8,128)(2,1)}, bf16[64,1024]{1,0:T(8,128)(2,1)S(1)}, u32[]{:S(2)}, u32[]{:S(2)}) collective-permute-start(bf16[64,1024]{1,0:T(8,128)(2,1)} %acts.3), channel_id=1, source_target_pairs={{0,8},{8,0},{1,9},{9,1},{2,10},{10,2},{3,11},{11,3},{4,12},{12,4},... | collective-permute-start | bytes 393224 | tf_op jit(solution)/shard_map/ppermute | solution.py:187
  3.8 5.8 %copy-start = (bf16[128,1024,64]{1,2,0:T(8,128)(2,1)S(1)}, bf16[128,1024,64]{1,2,0:T(8,128)(2,1)}, u32[]{:S(2)}) copy-start(bf16[128,1024,64]{1,2,0:T(8,128)(2,1)} %param.9) | copy-start | bytes 50331652
  9.6 5.8 %copy-start.1 = (bf16[128,64,1024]{2,1,0:T(8,128)(2,1)S(1)}, bf16[128,64,1024]{2,1,0:T(8,128)(2,1)}, u32[]{:S(2)}) copy-start(bf16[128,64,1024]{2,1,0:T(8,128)(2,1)} %up.1) | copy-start | bytes 50331652
  15.4 0.9 %copy-start.2 = (bf16[64,1024]{1,0:T(8,128)(2,1)S(1)}, bf16[64,1024]{1,0:T(8,128)(2,1)}, u32[]{:S(2)}) copy-start(bf16[64,1024]{1,0:T(8,128)(2,1)} %acts.3) | copy-start | bytes 393220
  16.3 0.7 %copy-start.4 = (s32[256]{0:T(256)S(1)}, s32[256]{0:T(256)}, u32[]{:S(2)}) copy-start(s32[256]{0:T(256)} %table.1) | copy-start | bytes 3076
  16.9 5.0 %copy-start.3 = (bf16[64,1024]{1,0:T(8,128)(2,1)S(1)}, bf16[64,1024]{1,0:T(8,128)(2,1)}, u32[]{:S(2)}) copy-start(bf16[64,1024]{1,0:T(8,128)(2,1)} %acts.3) | copy-start | bytes 393220

commit v3 on v2

--- a/solution.py
+++ b/solution.py
@@ -14,11 +14,12 @@
 HOPS = (2, 1, 3, 0)
 
 
-def pick_kernel(owned, wanted, table, acts, others, mask, down, up, shrunk, chosen, rows, down_sem, up_sem):
+def pick_kernel(owned, wanted, other_wanted, table, acts, others, down, up, shrunk, chosen, rows, down_sem, up_sem):
     me = lax.axis_index("replica")
-    count = wanted.shape[0]
-    half = count // 2
-    stored = [table[wanted[b]] for b in range(count)]
+    half = wanted.shape[0]
+    count = 2 * half
+    stored = [table[wanted[b]] for b in range(half)]
+    stored += [table[other_wanted[b]] for b in range(half)]
     copies = []
     for b in range(count):
         spot = lax.rem(stored[b], owned)
@@ -44,7 +45,7 @@
             )
             parts.append(part * (lax.div(stored[at], owned) == me).astype(F32))
         sides.append(jnp.concatenate(parts, axis=0))
-    shrunk[...] = jnp.concatenate(sides, axis=1) * mask[...]
+    shrunk[...] = jnp.concatenate(sides, axis=1)
     for _, second in copies:
         second.wait()
 
@@ -67,7 +68,7 @@
 
 
 def main_kernel(
-    acts, matrix, shrunk, chosen, out,
+    acts, matrix, shrunk, chosen, names, out,
     weights, x_out, x_in, z_out, z_in, s_pair, s_sum, s_in, total, d_out, d_in,
     w_sem, x_send, x_recv, z_send, z_recv, s_send, s_recv, d_send, d_recv,
 ):
@@ -154,10 +155,15 @@
     for b in range(half):
         d_out[b * step : (b + 1) * step, :] = delta(1, b)
     d_copy = send(d_out, d_in, d_send, d_recv, twin)
-    for b in range(half):
-        total[b * step : (b + 1) * step, :] += delta(0, b)
+    count = acts.shape[0]
+    same = lax.broadcasted_iota(jnp.int32, (count, count), 0) == lax.broadcasted_iota(
+        jnp.int32, (count, count), 1
+    )
+    named = jnp.broadcast_to((names[...] >= 0).astype(F32), (count, count))
+    alive = jnp.sum(jnp.where(same, named, 0.0), axis=1, keepdims=True)
+    own = jnp.concatenate([delta(0, b) for b in range(half)], axis=0)
     d_copy.wait_recv()
-    total[...] += d_in[...]
+    total[...] += (own + d_in[...]) * alive
     x_copies[3].wait_recv()
     total[...] += decode(x_in.at[3], width)
     for i in range(2):
@@ -182,12 +188,8 @@
     owned, _, rank = stored_down_factors.shape
     width = stored_up_factors.shape[2]
     half = adapter_per_block.shape[0]
-    names = jnp.concatenate([adapter_per_block, adapter_per_token])
-    other_names = lax.ppermute(names, "replica", [(0, 1), (1, 0)])
+    other_blocks = lax.ppermute(adapter_per_block, "replica", [(0, 1), (1, 0)])
     others = lax.ppermute(acts, "replica", [(0, 1), (1, 0)])
-    wanted = jnp.concatenate([adapter_per_block, other_names[:half]])
-    both = jnp.stack([adapter_per_token, other_names[half:]], axis=1)
-    mask = jnp.repeat((both >= 0).astype(F32), rank, axis=1)
     smem = pl.BlockSpec(memory_space=pltpu.SMEM)
     vmem = pl.BlockSpec(memory_space=pltpu.VMEM)
     anywhere = pl.BlockSpec(memory_space=pl.ANY)
@@ -197,17 +199,17 @@
             jax.ShapeDtypeStruct((rows, 2 * rank), F32),
             jax.ShapeDtypeStruct((2 * half, rank, width), jnp.bfloat16),
         ],
-        in_specs=[smem, smem, vmem, vmem, vmem, anywhere, anywhere],
+        in_specs=[smem, smem, smem, vmem, vmem, anywhere, anywhere],
         out_specs=[vmem, vmem],
         scratch_shapes=[
             pltpu.VMEM((2 * half, rank, features), jnp.bfloat16),
             pltpu.SemaphoreType.DMA((2 * half,)),
             pltpu.SemaphoreType.DMA((2 * half,)),
         ],
-        compiler_params=pltpu.CompilerParams(vmem_limit_bytes=16 * 2**20),
+        compiler_params=pltpu.CompilerParams(vmem_limit_bytes=50 * 2**20),
         name="pick",
     )(
-        wanted, adapter_storage_row, acts, others, mask,
+        adapter_per_block, other_blocks, adapter_storage_row, acts, others,
         jnp.swapaxes(stored_down_factors, 1, 2), stored_up_factors,
     )
     coded = (rows, width + TAIL)
@@ -215,7 +217,7 @@
     return pl.pallas_call(
         main_kernel,
         out_shape=jax.ShapeDtypeStruct((rows, width), jnp.bfloat16),
-        in_specs=[vmem, anywhere, vmem, vmem],
+        in_specs=[vmem, anywhere, vmem, vmem, vmem],
         out_specs=vmem,
         scratch_shapes=[
             pltpu.VMEM((8, features, width), jnp.bfloat16),
@@ -232,10 +234,10 @@
             dma((8,)), dma((4,)), dma((4,)), dma((3,)), dma((3,)), dma((4,)), dma((4,)), dma, dma,
         ],
         compiler_params=pltpu.CompilerParams(
-            collective_id=0, has_side_effects=True, vmem_limit_bytes=40 * 2**20
+            collective_id=0, has_side_effects=True, vmem_limit_bytes=50 * 2**20
         ),
         name="main",
-    )(acts, base_output_matrix, shrunk, chosen)
+    )(acts, base_output_matrix, shrunk, chosen, adapter_per_token.reshape(1, rows))
 
 
 def shards(

time: 49.3 us -> 34.4 us (0.70)
  local copies, waits for them, and re-layouts: 14.2 us -> 2.9 us
  other arithmetic: 2.14 us -> 0 us
  Pallas kernels: 31.4 us -> 29.6 us
    unnamed x11, local copies, waits for them, and re-layouts: 13.8 us -> 2.9 us
    pallas_call x1, Pallas kernels: 4.99 us -> 3.19 us  [kernel_shards(): pl.pallas_call(functools.partial(pick_kernel, owned), out_shape=[jax.Shap...]
    concatenate x2 -> x0, other arithmetic: 1.48 us -> none  [the longest x1 0.75 us: kernel_shards(): names = jnp.concatenate([adapter_per_block, adapter_per_token])]
    convert_element_type x1 -> x0, other arithmetic: 0.66 us -> none  [kernel_shards(): mask = jnp.repeat((both >= 0).astype(F32), rank, axis=1)]
  transfers between devices with their start and end apart: 2 -> 2, of which waited for: 1 -> 1; matrix products, arithmetic and copies ran while one was open for 4% -> 0% of each run, Pallas kernels for 0% -> 0%
where the time goes in v3:
time: 34.4 us; the launch traced here: 34.3 us
  Pallas kernels  29.6 us (86%)
  local copies, waits for them, and re-layouts  2.9 us (8%)
  waiting for transfers between devices  1.2 us (3%)
  starting transfers between devices  0.51 us (1%)
    pallas_call x1, Pallas kernels, kernel_shards(): pl.pallas_call(main_kernel, out_shape=jax.ShapeDtypeStruct((rows, width),...  26.4 us
    pallas_call x1, Pallas kernels, kernel_shards(): pl.pallas_call(functools.partial(pick_kernel, owned), out_shape=[jax.Shap...  3.19 us
    unnamed x11, local copies, waits for them, and re-layouts  2.9 us
    ppermute x1, waiting for transfers between devices, kernel_shards(): other_blocks = lax.ppermute(adapter_per_block, 'replica', [(0, 1), (1, 0)])  1.2 us
  transfers between devices with their start and end apart: 2, of which 1 were waited for; matrix products, arithmetic and copies ran while one was open for 0% of the time, Pallas kernels for 0%

profile of v3, /device:TPU:0, one launch (start us, length us, event | category | flops | bytes accessed | tf_op | source)
XLA Modules:
  0.0 34.3 jit_solution(9024062330142999973)
XLA Ops:
  0.0 0.5 %collective-permute-start.1 = (bf16[64,1024]{1,0:T(8,128)(2,1)}, bf16[64,1024]{1,0:T(8,128)(2,1)S(1)}, u32[]{:S(2)}, u32[]{:S(2)}) collective-permute-start(bf16[64,1024]{1,0:T(8,128)(2,1)} %acts.3), channel_id=1, source_target_pairs={{0,8},{8,0},{1,9},{9,1},{2,10},{10,2},{3,11},{11,3},{4,12},{12,4},... | collective-permute-start | bytes 393224 | tf_op jit(solution)/shard_map/ppermute | solution.py:192
  0.5 0.1 collective-permute-start
  0.5 1.2 %collective-permute-done.other_wanted = s32[4]{0:T(128)S(1)} collective-permute-done((s32[4]{0:T(128)}, s32[4]{0:T(128)S(1)}, u32[]{:S(2)}, u32[]{:S(2)}) %collective-permute-start) | collective-permute-done | bytes 48 | tf_op jit(solution)/shard_map/ppermute | solution.py:191
  1.7 0.0 collective-permute-done.1.others
  1.7 0.0 copy-start
  1.7 0.9 %copy-done = bf16[64,1024]{1,0:T(8,128)(2,1)S(1)} copy-done((bf16[64,1024]{1,0:T(8,128)(2,1)S(1)}, bf16[64,1024]{1,0:T(8,128)(2,1)}, u32[]{:S(2)}) %copy-start) | copy-done | bytes 131096
  2.6 0.0 copy-start.2
  2.6 0.7 %copy-done.2 = s32[256]{0:T(256)S(1)} copy-done((s32[256]{0:T(256)S(1)}, s32[256]{0:T(256)}, u32[]{:S(2)}) %copy-start.2) | copy-done | bytes 1048
  3.3 0.0 copy-start.3
  3.3 0.7 %copy-done.3 = s32[4]{0:T(128)S(1)} copy-done((s32[4]{0:T(128)S(1)}, s32[4]{0:T(128)}, u32[]{:S(2)}) %copy-start.3) | copy-done | bytes 40
  4.0 0.0 copy-start.1
  4.0 0.0 copy-start.4
  4.0 3.2 %pick.1 = (f32[64,128]{1,0:T(8,128)S(1)}, bf16[8,64,1024]{2,1,0:T(8,128)(2,1)S(1)}) custom-call(s32[4]{0:T(128)S(1)} %copy-done.3, s32[4]{0:T(128)S(1)} %collective-permute-done.other_wanted, s32[256]{0:T(256)S(1)} %copy-done.2, bf16[64,1024]{1,0:T(8,128)(2,1)S(1)} %copy-done, bf16[64,1024]{1,0:T(8,128)(2,1)S(1)} %collective-permute-done.1.others, ...), custom_call_target="tpu_custom_call" | custom-call | tf_op jit(solution)/shard_map/pick/pallas_call | solution.py:196
  7.2 0.0 copy-done.1
  7.2 0.0 copy-done.4
  7.2 26.4 %main.1 = bf16[64,1024]{1,0:T(8,128)(2,1)S(1)} custom-call(bf16[64,1024]{1,0:T(8,128)(2,1)S(1)} %copy-done.1, bf16[1024,8192]{1,0:T(8,128)(2,1)} %matrix.1, f32[64,128]{1,0:T(8,128)S(1)} %get-tuple-element.7.shrunk, bf16[8,64,1024]{2,1,0:T(8,128)(2,1)S(1)} %get-tuple-element.8.chosen, s32[1,64]{1,0:T(1,128)S(1)} %bitcast.2), custom_call_target="tpu_custom_call" | custom-call | tf_op jit(solution)/shard_map/main/pallas_call | solution.py:217
  33.6 0.7 %copy.9 = bf16[64,1024]{1,0:T(8,128)(2,1)} copy(bf16[64,1024]{1,0:T(8,128)(2,1)S(1)} %main.1) | data formatting | bytes 262144
Async XLA Ops:
  0.0 1.7 %collective-permute-start.1 = (bf16[64,1024]{1,0:T(8,128)(2,1)}, bf16[64,1024]{1,0:T(8,128)(2,1)S(1)}, u32[]{:S(2)}, u32[]{:S(2)}) collective-permute-start(bf16[64,1024]{1,0:T(8,128)(2,1)} %acts.3), channel_id=1, source_target_pairs={{0,8},{8,0},{1,9},{9,1},{2,10},{10,2},{3,11},{11,3},{4,12},{12,4},... | collective-permute-start | bytes 393224 | tf_op jit(solution)/shard_map/ppermute | solution.py:192
  0.5 1.3 %collective-permute-start = (s32[4]{0:T(128)}, s32[4]{0:T(128)S(1)}, u32[]{:S(2)}, u32[]{:S(2)}) collective-permute-start(s32[4]{0:T(128)} %wanted.1), channel_id=1, source_target_pairs={{0,8},{8,0},{1,9},{9,1},{2,10},{10,2},{3,11},{11,3},{4,12},{12,4},... | collective-permute-start | bytes 56 | tf_op jit(solution)/shard_map/ppermute | solution.py:191
  1.7 0.9 %copy-start = (bf16[64,1024]{1,0:T(8,128)(2,1)S(1)}, bf16[64,1024]{1,0:T(8,128)(2,1)}, u32[]{:S(2)}) copy-start(bf16[64,1024]{1,0:T(8,128)(2,1)} %acts.3) | copy-start | bytes 393220
  2.6 0.7 %copy-start.2 = (s32[256]{0:T(256)S(1)}, s32[256]{0:T(256)}, u32[]{:S(2)}) copy-start(s32[256]{0:T(256)} %table.1) | copy-start | bytes 3076
  3.3 0.7 %copy-start.3 = (s32[4]{0:T(128)S(1)}, s32[4]{0:T(128)}, u32[]{:S(2)}) copy-start(s32[4]{0:T(128)} %wanted.1) | copy-start | bytes 52
  4.0 3.2 %copy-start.1 = (bf16[64,1024]{1,0:T(8,128)(2,1)S(1)}, bf16[64,1024]{1,0:T(8,128)(2,1)}, u32[]{:S(2)}) copy-start(bf16[64,1024]{1,0:T(8,128)(2,1)} %acts.3) | copy-start | bytes 393220
  4.0 3.2 %copy-start.4 = (s32[64]{0:T(128)S(1)}, s32[64]{0:T(128)}, u32[]{:S(2)}) copy-start(s32[64]{0:T(128)} %param.13) | copy-start | bytes 772

commit v4 on v3

--- a/solution.py
+++ b/solution.py
@@ -11,7 +11,7 @@
 F32 = jnp.float32
 TAIL = 128
 LEVELS = 32000.0
-HOPS = (2, 1, 3, 0)
+ROWS = 16
 
 
 def pick_kernel(owned, wanted, other_wanted, table, acts, others, down, up, shrunk, chosen, rows, down_sem, up_sem):
@@ -51,23 +51,56 @@
 
 
 def encode(value, slot):
-    width = value.shape[1]
+    count, width = value.shape
     largest = jnp.maximum(jnp.max(jnp.abs(value), axis=1, keepdims=True), 1e-30)
-    level = jnp.ceil(jnp.log2(largest))
-    factor = jnp.exp2(-level) * LEVELS
+    level = jnp.ceil(jnp.log2(largest) * 4.0)
+    factor = jnp.exp2(level * -0.25) * LEVELS
     coded = jnp.round(jnp.clip(value * factor, -32767.0, 32767.0))
-    slot[:, 0:width] = coded.astype(jnp.int32).astype(jnp.int16)
-    slot[:, width : width + TAIL] = (
-        jnp.broadcast_to(level, (value.shape[0], TAIL)).astype(jnp.int32).astype(jnp.int16)
-    )
+    coded = coded.astype(jnp.int32).astype(jnp.int16)
+    for i in range(count // ROWS):
+        slot[:, i * width : (i + 1) * width] = coded[i * ROWS : (i + 1) * ROWS, :]
+    row = jnp.sum(jnp.where(diagonal(count), level, 0.0), axis=0, keepdims=True)
+    tail = count // ROWS * width
+    slot[:, tail : tail + TAIL] = (
+        jnp.broadcast_to(row, (ROWS, TAIL)).astype(jnp.int32).astype(jnp.int16)
+    )
+
+
+def diagonal(count):
+    shape = (count, TAIL)
+    return lax.broadcasted_iota(jnp.int32, shape, 0) == lax.broadcasted_iota(jnp.int32, shape, 1)
 
 
 def decode(slot, width):
-    level = slot[:, width : width + TAIL].astype(jnp.int32).astype(F32)[:, 0:1]
-    return slot[:, 0:width].astype(jnp.int32).astype(F32) * (jnp.exp2(level) * (1.0 / LEVELS))
-
-
-def main_kernel(
+    folds = slot.shape[1] // width
+    tail = folds * width
+    row = slot[:, tail : tail + TAIL].astype(jnp.int32).astype(F32)[0:1, :]
+    count = folds * ROWS
+    level = jnp.sum(
+        jnp.where(diagonal(count), jnp.broadcast_to(row, (count, TAIL)), 0.0), axis=1, keepdims=True
+    )
+    values = jnp.concatenate(
+        [slot[:, i * width : (i + 1) * width].astype(jnp.int32).astype(F32) for i in range(folds)],
+        axis=0,
+    )
+    return values * (jnp.exp2(level * 0.25) * (1.0 / LEVELS))
+
+
+def main_kernel(*refs):
+    z = lax.div(lax.axis_index("tensor"), 2)
+    edge = jnp.logical_or(z == 0, z == 3)
+
+    @pl.when(edge)
+    def _():
+        run(True, z, *refs)
+
+    @pl.when(jnp.logical_not(edge))
+    def _():
+        run(False, z, *refs)
+
+
+def run(
+    edge, z,
     acts, matrix, shrunk, chosen, names, out,
     weights, x_out, x_in, z_out, z_in, s_pair, s_sum, s_in, total, d_out, d_in,
     w_sem, x_send, x_recv, z_send, z_recv, s_send, s_recv, d_send, d_recv,
@@ -75,17 +108,30 @@
     g = lax.axis_index("groups")
     r = lax.axis_index("replica")
     t = lax.axis_index("tensor")
-    z, x = lax.div(t, 2), lax.rem(t, 2)
+    x = lax.rem(t, 2)
     width = out.shape[1]
-    far = [lax.rem(z + k, 4) for k in HOPS]
+    if edge:
+        near = 1 + lax.div(z, 3)
+        order = [3 - near, 3 - z, near, z]
+        hops = [near, near, near]
+        slots = [0, 1, 2]
+    else:
+        near = 3 * (z - 1)
+        order = [near, 3 - z, 3 - near, z]
+        hops = [near, 3 - z, 3 - near]
+        slots = [0, 3, 1]
+
+    def peer(at):
+        return (g, r, 2 * at + x)
+
     pair = (g, r, 2 * z + (1 - x))
-    peers = [(g, r, 2 * far[i] + x) for i in range(3)]
     twin = (g, 1 - r, t)
+    peers = [peer(lax.rem(z + k, 4)) for k in (1, 2, 3)]
 
     loads = []
     for i in range(4):
         for j, column in enumerate((1 - x, x)):
-            place = pl.multiple_of((2 * far[i] + column) * width, width)
+            place = pl.multiple_of((2 * order[i] + column) * width, width)
             loads.append(
                 pltpu.make_async_copy(
                     matrix.at[:, pl.ds(place, width)], weights.at[2 * i + j], w_sem.at[2 * i + j]
@@ -99,17 +145,24 @@
         pl.semaphore_signal(barrier, inc=1, device_id=device, device_id_type=MESH)
     pl.semaphore_wait(barrier, 5)
 
-    def send(source, target, one, two, device):
-        copy = pltpu.make_async_remote_copy(
+    def remote(source, target, one, two, device):
+        return pltpu.make_async_remote_copy(
             src_ref=source, dst_ref=target, send_sem=one, recv_sem=two,
             device_id=device, device_id_type=MESH,
         )
+
+    def send(*what):
+        copy = remote(*what)
         copy.start()
         return copy
 
     def product(at):
         loads[at].wait()
         return jnp.dot(acts[...], weights[at], preferred_element_type=F32)
+
+    def arrived(slot):
+        remote(z_out.at[0], z_in.at[slot], z_send.at[0], z_recv.at[slot], peers[0]).wait_recv()
+        return decode(z_in.at[slot], width)
 
     s_copies = [send(shrunk, s_pair, s_send.at[3], s_recv.at[3], pair)]
     x_copies = []
@@ -130,8 +183,13 @@
             x_step(i + 2)
         mine = product(2 * i + 1)
         x_copies[i].wait_recv()
-        encode(mine + decode(x_in.at[i], width), z_out.at[i])
-        z_copies.append(send(z_out.at[i], z_in.at[i], z_send.at[i], z_recv.at[i], peers[i]))
+        mine = mine + decode(x_in.at[i], width)
+        if not edge and i:
+            mine = mine + arrived(i - 1)
+        encode(mine, z_out.at[i])
+        z_copies.append(
+            send(z_out.at[i], z_in.at[slots[i]], z_send.at[i], z_recv.at[slots[i]], peer(hops[i]))
+        )
     total[...] = product(7)
 
     for copy in s_copies[1:]:
@@ -143,7 +201,8 @@
     low = (rest - middle.astype(F32)).astype(jnp.bfloat16)
     half = chosen.shape[0] // 2
     rank = chosen.shape[1]
-    step = acts.shape[0] // half
+    count = acts.shape[0]
+    step = count // half
 
     def delta(side, b):
         rows = slice(b * step, (b + 1) * step)
@@ -155,7 +214,6 @@
     for b in range(half):
         d_out[b * step : (b + 1) * step, :] = delta(1, b)
     d_copy = send(d_out, d_in, d_send, d_recv, twin)
-    count = acts.shape[0]
     same = lax.broadcasted_iota(jnp.int32, (count, count), 0) == lax.broadcasted_iota(
         jnp.int32, (count, count), 1
     )
@@ -166,11 +224,13 @@
     total[...] += (own + d_in[...]) * alive
     x_copies[3].wait_recv()
     total[...] += decode(x_in.at[3], width)
-    for i in range(2):
-        z_copies[i].wait_recv()
-        total[...] += decode(z_in.at[i], width)
-    z_copies[2].wait_recv()
-    out[...] = (total[...] + decode(z_in.at[2], width)).astype(out.dtype)
+    if edge:
+        total[...] += arrived(0)
+        last = 1
+    else:
+        total[...] += arrived(2)
+        last = 3
+    out[...] = (total[...] + arrived(last)).astype(out.dtype)
     for copy in s_copies + x_copies + z_copies + [d_copy]:
         copy.wait_send()
 
@@ -212,7 +272,7 @@
         adapter_per_block, other_blocks, adapter_storage_row, acts, others,
         jnp.swapaxes(stored_down_factors, 1, 2), stored_up_factors,
     )
-    coded = (rows, width + TAIL)
+    coded = (ROWS, rows // ROWS * width + TAIL)
     dma = pltpu.SemaphoreType.DMA
     return pl.pallas_call(
         main_kernel,
@@ -224,14 +284,14 @@
             pltpu.VMEM((4,) + coded, jnp.int16),
             pltpu.VMEM((4,) + coded, jnp.int16),
             pltpu.VMEM((3,) + coded, jnp.int16),
-            pltpu.VMEM((3,) + coded, jnp.int16),
+            pltpu.VMEM((4,) + coded, jnp.int16),
             pltpu.VMEM((rows, 2 * rank), F32),
             pltpu.VMEM((rows, 2 * rank), F32),
             pltpu.VMEM((3, rows, 2 * rank), F32),
             pltpu.VMEM((rows, width), F32),
             pltpu.VMEM((rows, width), F32),
             pltpu.VMEM((rows, width), F32),
-            dma((8,)), dma((4,)), dma((4,)), dma((3,)), dma((3,)), dma((4,)), dma((4,)), dma, dma,
+            dma((8,)), dma((4,)), dma((4,)), dma((3,)), dma((4,)), dma((4,)), dma((4,)), dma, dma,
         ],
         compiler_params=pltpu.CompilerParams(
             collective_id=0, has_side_effects=True, vmem_limit_bytes=50 * 2**20

time: 34.4 us -> 31.8 us (0.924)
  Pallas kernels: 29.6 us -> 26.9 us
    pallas_call x1, Pallas kernels: 26.4 us -> 23.8 us  [kernel_shards(): pl.pallas_call(main_kernel, out_shape=jax.ShapeDtypeStruct((rows, width),...]
where the time goes in v4:
time: 31.8 us; the launch traced here: 31.6 us
  Pallas kernels  26.9 us (85%)
  local copies, waits for them, and re-layouts  2.9 us (9%)
  waiting for transfers between devices  1.2 us (4%)
  starting transfers between devices  0.51 us (2%)
    pallas_call x1, Pallas kernels, kernel_shards(): pl.pallas_call(main_kernel, out_shape=jax.ShapeDtypeStruct((rows, width),...  23.8 us
    pallas_call x1, Pallas kernels, kernel_shards(): pl.pallas_call(functools.partial(pick_kernel, owned), out_shape=[jax.Shap...  3.19 us
    unnamed x11, local copies, waits for them, and re-layouts  2.9 us
    ppermute x1, waiting for transfers between devices, kernel_shards(): other_blocks = lax.ppermute(adapter_per_block, 'replica', [(0, 1), (1, 0)])  1.2 us
  transfers between devices with their start and end apart: 2, of which 1 were waited for; matrix products, arithmetic and copies ran while one was open for 0% of the time, Pallas kernels for 0%

profile of v4, /device:TPU:0, one launch (start us, length us, event | category | flops | bytes accessed | tf_op | source)
XLA Modules:
  0.0 31.6 jit_solution(4075033810239105884)
XLA Ops:
  0.0 0.5 %collective-permute-start.1 = (bf16[64,1024]{1,0:T(8,128)(2,1)}, bf16[64,1024]{1,0:T(8,128)(2,1)S(1)}, u32[]{:S(2)}, u32[]{:S(2)}) collective-permute-start(bf16[64,1024]{1,0:T(8,128)(2,1)} %refs_0_.1), channel_id=1, source_target_pairs={{0,8},{8,0},{1,9},{9,1},{2,10},{10,2},{3,11},{11,3},{4,12},{12,4},... | collective-permute-start | bytes 393224 | tf_op jit(solution)/shard_map/ppermute | solution.py:252
  0.5 0.1 collective-permute-start
  0.5 1.2 %collective-permute-done.other_wanted = s32[4]{0:T(128)S(1)} collective-permute-done((s32[4]{0:T(128)}, s32[4]{0:T(128)S(1)}, u32[]{:S(2)}, u32[]{:S(2)}) %collective-permute-start) | collective-permute-done | bytes 48 | tf_op jit(solution)/shard_map/ppermute | solution.py:251
  1.7 0.0 collective-permute-done.1.others
  1.7 0.0 copy-start
  1.7 0.9 %copy-done = bf16[64,1024]{1,0:T(8,128)(2,1)S(1)} copy-done((bf16[64,1024]{1,0:T(8,128)(2,1)S(1)}, bf16[64,1024]{1,0:T(8,128)(2,1)}, u32[]{:S(2)}) %copy-start) | copy-done | bytes 131096
  2.6 0.0 copy-start.2
  2.6 0.7 %copy-done.2 = s32[256]{0:T(256)S(1)} copy-done((s32[256]{0:T(256)S(1)}, s32[256]{0:T(256)}, u32[]{:S(2)}) %copy-start.2) | copy-done | bytes 1048
  3.3 0.0 copy-start.3
  3.3 0.7 %copy-done.3 = s32[4]{0:T(128)S(1)} copy-done((s32[4]{0:T(128)S(1)}, s32[4]{0:T(128)}, u32[]{:S(2)}) %copy-start.3) | copy-done | bytes 40
  4.0 0.0 copy-start.1
  4.0 0.0 copy-start.4
  4.0 3.2 %pick.1 = (f32[64,128]{1,0:T(8,128)S(1)}, bf16[8,64,1024]{2,1,0:T(8,128)(2,1)S(1)}) custom-call(s32[4]{0:T(128)S(1)} %copy-done.3, s32[4]{0:T(128)S(1)} %collective-permute-done.other_wanted, s32[256]{0:T(256)S(1)} %copy-done.2, bf16[64,1024]{1,0:T(8,128)(2,1)S(1)} %copy-done, bf16[64,1024]{1,0:T(8,128)(2,1)S(1)} %collective-permute-done.1.others, ...), custom_call_target="tpu_custom_call" | custom-call | tf_op jit(solution)/shard_map/pick/pallas_call | solution.py:256
  7.2 0.0 copy-done.1
  7.2 0.0 copy-done.4
  7.2 23.8 %main.1 = bf16[64,1024]{1,0:T(8,128)(2,1)S(1)} custom-call(bf16[64,1024]{1,0:T(8,128)(2,1)S(1)} %copy-done.1, bf16[1024,8192]{1,0:T(8,128)(2,1)} %refs_1_.1, f32[64,128]{1,0:T(8,128)S(1)} %get-tuple-element.7.refs_2_, bf16[8,64,1024]{2,1,0:T(8,128)(2,1)S(1)} %get-tuple-element.8.refs_3_, s32[1,64]{1,0:T(1,128)S(1)} %bitcast.2), custom_call_target="tpu_custom_call" | custom-call | tf_op jit(solution)/shard_map/main/pallas_call | solution.py:277
  30.9 0.7 %copy.9 = bf16[64,1024]{1,0:T(8,128)(2,1)} copy(bf16[64,1024]{1,0:T(8,128)(2,1)S(1)} %main.1) | data formatting | bytes 262144
Async XLA Ops:
  0.0 1.7 %collective-permute-start.1 = (bf16[64,1024]{1,0:T(8,128)(2,1)}, bf16[64,1024]{1,0:T(8,128)(2,1)S(1)}, u32[]{:S(2)}, u32[]{:S(2)}) collective-permute-start(bf16[64,1024]{1,0:T(8,128)(2,1)} %refs_0_.1), channel_id=1, source_target_pairs={{0,8},{8,0},{1,9},{9,1},{2,10},{10,2},{3,11},{11,3},{4,12},{12,4},... | collective-permute-start | bytes 393224 | tf_op jit(solution)/shard_map/ppermute | solution.py:252
  0.5 1.3 %collective-permute-start = (s32[4]{0:T(128)}, s32[4]{0:T(128)S(1)}, u32[]{:S(2)}, u32[]{:S(2)}) collective-permute-start(s32[4]{0:T(128)} %wanted.1), channel_id=1, source_target_pairs={{0,8},{8,0},{1,9},{9,1},{2,10},{10,2},{3,11},{11,3},{4,12},{12,4},... | collective-permute-start | bytes 56 | tf_op jit(solution)/shard_map/ppermute | solution.py:251
  1.7 0.9 %copy-start = (bf16[64,1024]{1,0:T(8,128)(2,1)S(1)}, bf16[64,1024]{1,0:T(8,128)(2,1)}, u32[]{:S(2)}) copy-start(bf16[64,1024]{1,0:T(8,128)(2,1)} %refs_0_.1) | copy-start | bytes 393220
  2.6 0.7 %copy-start.2 = (s32[256]{0:T(256)S(1)}, s32[256]{0:T(256)}, u32[]{:S(2)}) copy-start(s32[256]{0:T(256)} %table.1) | copy-start | bytes 3076
  3.3 0.7 %copy-start.3 = (s32[4]{0:T(128)S(1)}, s32[4]{0:T(128)}, u32[]{:S(2)}) copy-start(s32[4]{0:T(128)} %wanted.1) | copy-start | bytes 52
  4.0 3.2 %copy-start.1 = (bf16[64,1024]{1,0:T(8,128)(2,1)S(1)}, bf16[64,1024]{1,0:T(8,128)(2,1)}, u32[]{:S(2)}) copy-start(bf16[64,1024]{1,0:T(8,128)(2,1)} %refs_0_.1) | copy-start | bytes 393220
  4.0 3.2 %copy-start.4 = (s32[64]{0:T(128)S(1)}, s32[64]{0:T(128)}, u32[]{:S(2)}) copy-start(s32[64]{0:T(128)} %param.13) | copy-start | bytes 772

commit v5 on v4

--- a/solution.py
+++ b/solution.py
@@ -12,9 +12,24 @@
 TAIL = 128
 LEVELS = 32000.0
 ROWS = 16
-
-
-def pick_kernel(owned, wanted, other_wanted, table, acts, others, down, up, shrunk, chosen, rows, down_sem, up_sem):
+USED = (0, 2, 4, 1, 6, 3, 5, 7)
+AHEAD = 2
+
+
+def pick_kernel(
+    owned, wanted_in, other_in, table_in, acts_in, others, down, up, shrunk, chosen,
+    wanted, other_wanted, table, acts, rows, in_sem, down_sem, up_sem,
+):
+    inputs = [
+        pltpu.make_async_copy(source, target, in_sem.at[i])
+        for i, (source, target) in enumerate(
+            ((wanted_in, wanted), (other_in, other_wanted), (table_in, table), (acts_in, acts))
+        )
+    ]
+    for copy in inputs:
+        copy.start()
+    for copy in inputs[:3]:
+        copy.wait()
     me = lax.axis_index("replica")
     half = wanted.shape[0]
     count = 2 * half
@@ -31,6 +46,7 @@
     for _, second in copies:
         second.start()
     step = acts.shape[0] // half
+    inputs[3].wait()
     sides = []
     for side, source in ((0, acts), (1, others)):
         parts = []
@@ -137,7 +153,8 @@
                     matrix.at[:, pl.ds(place, width)], weights.at[2 * i + j], w_sem.at[2 * i + j]
                 )
             )
-    for load in loads:
+    ready = [loads[i] for i in USED]
+    for load in ready[:AHEAD]:
         load.start()
 
     barrier = pltpu.get_barrier_semaphore()
@@ -158,6 +175,9 @@
 
     def product(at):
         loads[at].wait()
+        later = USED.index(at) + AHEAD
+        if later < len(USED):
+            ready[later].start()
         return jnp.dot(acts[...], weights[at], preferred_element_type=F32)
 
     def arrived(slot):
@@ -250,7 +270,7 @@
     half = adapter_per_block.shape[0]
     other_blocks = lax.ppermute(adapter_per_block, "replica", [(0, 1), (1, 0)])
     others = lax.ppermute(acts, "replica", [(0, 1), (1, 0)])
-    smem = pl.BlockSpec(memory_space=pltpu.SMEM)
+    hbm = pl.BlockSpec(memory_space=pltpu.HBM)
     vmem = pl.BlockSpec(memory_space=pltpu.VMEM)
     anywhere = pl.BlockSpec(memory_space=pl.ANY)
     shrunk, chosen = pl.pallas_call(
@@ -259,10 +279,15 @@
             jax.ShapeDtypeStruct((rows, 2 * rank), F32),
             jax.ShapeDtypeStruct((2 * half, rank, width), jnp.bfloat16),
         ],
-        in_specs=[smem, smem, smem, vmem, vmem, anywhere, anywhere],
+        in_specs=[hbm, vmem, hbm, hbm, vmem, anywhere, anywhere],
         out_specs=[vmem, vmem],
         scratch_shapes=[
+            pltpu.SMEM(adapter_per_block.shape, jnp.int32),
+            pltpu.SMEM(adapter_per_block.shape, jnp.int32),
+            pltpu.SMEM(adapter_storage_row.shape, jnp.int32),
+            pltpu.VMEM(acts.shape, jnp.bfloat16),
             pltpu.VMEM((2 * half, rank, features), jnp.bfloat16),
+            pltpu.SemaphoreType.DMA((4,)),
             pltpu.SemaphoreType.DMA((2 * half,)),
             pltpu.SemaphoreType.DMA((2 * half,)),
         ],

time: 31.8 us -> 31.8 us (level)
  no operation moved by 1% of the time
where the time goes in v5:
time: 31.8 us; the launch traced here: 31.6 us
  Pallas kernels  27 us (85%)
  local copies, waits for them, and re-layouts  2.9 us (9%)
  waiting for transfers between devices  1.2 us (4%)
  starting transfers between devices  0.51 us (2%)
    pallas_call x1, Pallas kernels, kernel_shards(): pl.pallas_call(main_kernel, out_shape=jax.ShapeDtypeStruct((rows, width),...  23.8 us
    pallas_call x1, Pallas kernels, kernel_shards(): pl.pallas_call(functools.partial(pick_kernel, owned), out_shape=[jax.Shap...  3.22 us
    unnamed x11, local copies, waits for them, and re-layouts  2.9 us
    ppermute x1, waiting for transfers between devices, kernel_shards(): other_blocks = lax.ppermute(adapter_per_block, 'replica', [(0, 1), (1, 0)])  1.2 us
  transfers between devices with their start and end apart: 2, of which 1 were waited for; matrix products, arithmetic and copies ran while one was open for 0% of the time, Pallas kernels for 0%

profile of v5, /device:TPU:0, one launch (start us, length us, event | category | flops | bytes accessed | tf_op | source)
XLA Modules:
  0.0 31.6 jit_solution(12024974535449462727)
XLA Ops:
  0.0 0.5 %collective-permute-start.1 = (bf16[64,1024]{1,0:T(8,128)(2,1)}, bf16[64,1024]{1,0:T(8,128)(2,1)S(1)}, u32[]{:S(2)}, u32[]{:S(2)}) collective-permute-start(bf16[64,1024]{1,0:T(8,128)(2,1)} %refs_0_.1), channel_id=1, source_target_pairs={{0,8},{8,0},{1,9},{9,1},{2,10},{10,2},{3,11},{11,3},{4,12},{12,4},... | collective-permute-start | bytes 393224 | tf_op jit(solution)/shard_map/ppermute | solution.py:272
  0.5 0.1 collective-permute-start
  0.5 1.2 %collective-permute-done.other_in = s32[4]{0:T(128)S(1)} collective-permute-done((s32[4]{0:T(128)}, s32[4]{0:T(128)S(1)}, u32[]{:S(2)}, u32[]{:S(2)}) %collective-permute-start) | collective-permute-done | bytes 48 | tf_op jit(solution)/shard_map/ppermute | solution.py:271
  1.7 0.0 collective-permute-done.1.others
  1.7 0.0 copy-start
  1.7 0.9 %copy-done = bf16[64,1024]{1,0:T(8,128)(2,1)S(1)} copy-done((bf16[64,1024]{1,0:T(8,128)(2,1)S(1)}, bf16[64,1024]{1,0:T(8,128)(2,1)}, u32[]{:S(2)}) %copy-start) | copy-done | bytes 131096
  2.6 0.0 copy-start.2
  2.6 0.7 %copy-done.2 = s32[256]{0:T(256)S(1)} copy-done((s32[256]{0:T(256)S(1)}, s32[256]{0:T(256)}, u32[]{:S(2)}) %copy-start.2) | copy-done | bytes 1048
  3.3 0.0 copy-start.3
  3.3 0.7 %copy-done.3 = s32[4]{0:T(128)S(1)} copy-done((s32[4]{0:T(128)S(1)}, s32[4]{0:T(128)}, u32[]{:S(2)}) %copy-start.3) | copy-done | bytes 40
  4.0 0.0 copy-start.1
  4.0 0.0 copy-start.4
  4.0 3.2 %pick.1 = (f32[64,128]{1,0:T(8,128)S(1)}, bf16[8,64,1024]{2,1,0:T(8,128)(2,1)S(1)}) custom-call(s32[4]{0:T(128)S(1)} %copy-done.3, s32[4]{0:T(128)S(1)} %collective-permute-done.other_in, s32[256]{0:T(256)S(1)} %copy-done.2, bf16[64,1024]{1,0:T(8,128)(2,1)S(1)} %copy-done, bf16[64,1024]{1,0:T(8,128)(2,1)S(1)} %collective-permute-done.1.others, ...), custom_call_target="tpu_custom_call" | custom-call | tf_op jit(solution)/shard_map/pick/pallas_call | solution.py:276
  7.2 0.0 copy-done.1
  7.2 0.0 copy-done.4
  7.2 23.8 %main.1 = bf16[64,1024]{1,0:T(8,128)(2,1)S(1)} custom-call(bf16[64,1024]{1,0:T(8,128)(2,1)S(1)} %copy-done.1, bf16[1024,8192]{1,0:T(8,128)(2,1)} %refs_1_.1, f32[64,128]{1,0:T(8,128)S(1)} %get-tuple-element.7.refs_2_, bf16[8,64,1024]{2,1,0:T(8,128)(2,1)S(1)} %get-tuple-element.8.refs_3_, s32[1,64]{1,0:T(1,128)S(1)} %bitcast.2), custom_call_target="tpu_custom_call" | custom-call | tf_op jit(solution)/shard_map/main/pallas_call | solution.py:302
  31.0 0.7 %copy.9 = bf16[64,1024]{1,0:T(8,128)(2,1)} copy(bf16[64,1024]{1,0:T(8,128)(2,1)S(1)} %main.1) | data formatting | bytes 262144
Async XLA Ops:
  0.0 1.7 %collective-permute-start.1 = (bf16[64,1024]{1,0:T(8,128)(2,1)}, bf16[64,1024]{1,0:T(8,128)(2,1)S(1)}, u32[]{:S(2)}, u32[]{:S(2)}) collective-permute-start(bf16[64,1024]{1,0:T(8,128)(2,1)} %refs_0_.1), channel_id=1, source_target_pairs={{0,8},{8,0},{1,9},{9,1},{2,10},{10,2},{3,11},{11,3},{4,12},{12,4},... | collective-permute-start | bytes 393224 | tf_op jit(solution)/shard_map/ppermute | solution.py:272
  0.5 1.3 %collective-permute-start = (s32[4]{0:T(128)}, s32[4]{0:T(128)S(1)}, u32[]{:S(2)}, u32[]{:S(2)}) collective-permute-start(s32[4]{0:T(128)} %wanted_in.1), channel_id=1, source_target_pairs={{0,8},{8,0},{1,9},{9,1},{2,10},{10,2},{3,11},{11,3},{4,12},{12,4},... | collective-permute-start | bytes 56 | tf_op jit(solution)/shard_map/ppermute | solution.py:271
  1.7 0.9 %copy-start = (bf16[64,1024]{1,0:T(8,128)(2,1)S(1)}, bf16[64,1024]{1,0:T(8,128)(2,1)}, u32[]{:S(2)}) copy-start(bf16[64,1024]{1,0:T(8,128)(2,1)} %refs_0_.1) | copy-start | bytes 393220
  2.6 0.7 %copy-start.2 = (s32[256]{0:T(256)S(1)}, s32[256]{0:T(256)}, u32[]{:S(2)}) copy-start(s32[256]{0:T(256)} %table_in.1) | copy-start | bytes 3076
  3.3 0.7 %copy-start.3 = (s32[4]{0:T(128)S(1)}, s32[4]{0:T(128)}, u32[]{:S(2)}) copy-start(s32[4]{0:T(128)} %wanted_in.1) | copy-start | bytes 52
  4.0 3.2 %copy-start.1 = (bf16[64,1024]{1,0:T(8,128)(2,1)S(1)}, bf16[64,1024]{1,0:T(8,128)(2,1)}, u32[]{:S(2)}) copy-start(bf16[64,1024]{1,0:T(8,128)(2,1)} %refs_0_.1) | copy-start | bytes 393220
  4.0 3.2 %copy-start.4 = (s32[64]{0:T(128)S(1)}, s32[64]{0:T(128)}, u32[]{:S(2)}) copy-start(s32[64]{0:T(128)} %param.13) | copy-start | bytes 772

commit v6 on v5

--- a/solution.py
+++ b/solution.py
@@ -144,6 +144,10 @@
     twin = (g, 1 - r, t)
     peers = [peer(lax.rem(z + k, 4)) for k in (1, 2, 3)]
 
+    barrier = pltpu.get_barrier_semaphore()
+    for device in [pair, twin] + peers:
+        pl.semaphore_signal(barrier, inc=1, device_id=device, device_id_type=MESH)
+
     loads = []
     for i in range(4):
         for j, column in enumerate((1 - x, x)):
@@ -157,11 +161,6 @@
     for load in ready[:AHEAD]:
         load.start()
 
-    barrier = pltpu.get_barrier_semaphore()
-    for device in [pair, twin] + peers:
-        pl.semaphore_signal(barrier, inc=1, device_id=device, device_id_type=MESH)
-    pl.semaphore_wait(barrier, 5)
-
     def remote(source, target, one, two, device):
         return pltpu.make_async_remote_copy(
             src_ref=source, dst_ref=target, send_sem=one, recv_sem=two,
@@ -184,12 +183,15 @@
         remote(z_out.at[0], z_in.at[slot], z_send.at[0], z_recv.at[slot], peers[0]).wait_recv()
         return decode(z_in.at[slot], width)
 
+    encode(product(0), x_out.at[0])
+    pl.semaphore_wait(barrier, 5)
     s_copies = [send(shrunk, s_pair, s_send.at[3], s_recv.at[3], pair)]
     x_copies = []
     z_copies = []
 
     def x_step(i):
-        encode(product(2 * i), x_out.at[i])
+        if i:
+            encode(product(2 * i), x_out.at[i])
         x_copies.append(send(x_out.at[i], x_in.at[i], x_send.at[i], x_recv.at[i], pair))
 
     x_step(0)

time: 31.8 us -> 32.5 us (1.022)
  Pallas kernels: 27 us -> 27.7 us
    pallas_call x1, Pallas kernels: 23.8 us -> 24.5 us  [kernel_shards(): pl.pallas_call(main_kernel, out_shape=jax.ShapeDtypeStruct((rows, width),...]
where the time goes in v6:
time: 32.5 us; the launch traced here: 32.4 us
  Pallas kernels  27.7 us (85%)
  local copies, waits for them, and re-layouts  2.9 us (9%)
  waiting for transfers between devices  1.2 us (4%)
  starting transfers between devices  0.51 us (2%)
    pallas_call x1, Pallas kernels, kernel_shards(): pl.pallas_call(main_kernel, out_shape=jax.ShapeDtypeStruct((rows, width),...  24.5 us
    pallas_call x1, Pallas kernels, kernel_shards(): pl.pallas_call(functools.partial(pick_kernel, owned), out_shape=[jax.Shap...  3.22 us
    unnamed x11, local copies, waits for them, and re-layouts  2.9 us
    ppermute x1, waiting for transfers between devices, kernel_shards(): other_blocks = lax.ppermute(adapter_per_block, 'replica', [(0, 1), (1, 0)])  1.2 us
  transfers between devices with their start and end apart: 2, of which 1 were waited for; matrix products, arithmetic and copies ran while one was open for 0% of the time, Pallas kernels for 0%

profile of v6, /device:TPU:0, one launch (start us, length us, event | category | flops | bytes accessed | tf_op | source)
XLA Modules:
  0.0 32.4 jit_solution(7901525073396495830)
XLA Ops:
  0.0 0.5 %collective-permute-start.1 = (bf16[64,1024]{1,0:T(8,128)(2,1)}, bf16[64,1024]{1,0:T(8,128)(2,1)S(1)}, u32[]{:S(2)}, u32[]{:S(2)}) collective-permute-start(bf16[64,1024]{1,0:T(8,128)(2,1)} %refs_0_.1), channel_id=1, source_target_pairs={{0,8},{8,0},{1,9},{9,1},{2,10},{10,2},{3,11},{11,3},{4,12},{12,4},... | collective-permute-start | bytes 393224 | tf_op jit(solution)/shard_map/ppermute | solution.py:274
  0.5 0.1 collective-permute-start
  0.5 1.2 %collective-permute-done.other_in = s32[4]{0:T(128)S(1)} collective-permute-done((s32[4]{0:T(128)}, s32[4]{0:T(128)S(1)}, u32[]{:S(2)}, u32[]{:S(2)}) %collective-permute-start) | collective-permute-done | bytes 48 | tf_op jit(solution)/shard_map/ppermute | solution.py:273
  1.7 0.0 collective-permute-done.1.others
  1.7 0.0 copy-start
  1.7 0.9 %copy-done = bf16[64,1024]{1,0:T(8,128)(2,1)S(1)} copy-done((bf16[64,1024]{1,0:T(8,128)(2,1)S(1)}, bf16[64,1024]{1,0:T(8,128)(2,1)}, u32[]{:S(2)}) %copy-start) | copy-done | bytes 131096
  2.6 0.0 copy-start.2
  2.6 0.7 %copy-done.2 = s32[256]{0:T(256)S(1)} copy-done((s32[256]{0:T(256)S(1)}, s32[256]{0:T(256)}, u32[]{:S(2)}) %copy-start.2) | copy-done | bytes 1048
  3.3 0.0 copy-start.3
  3.3 0.7 %copy-done.3 = s32[4]{0:T(128)S(1)} copy-done((s32[4]{0:T(128)S(1)}, s32[4]{0:T(128)}, u32[]{:S(2)}) %copy-start.3) | copy-done | bytes 40
  4.0 0.0 copy-start.1
  4.0 0.0 copy-start.4
  4.0 3.2 %pick.1 = (f32[64,128]{1,0:T(8,128)S(1)}, bf16[8,64,1024]{2,1,0:T(8,128)(2,1)S(1)}) custom-call(s32[4]{0:T(128)S(1)} %copy-done.3, s32[4]{0:T(128)S(1)} %collective-permute-done.other_in, s32[256]{0:T(256)S(1)} %copy-done.2, bf16[64,1024]{1,0:T(8,128)(2,1)S(1)} %copy-done, bf16[64,1024]{1,0:T(8,128)(2,1)S(1)} %collective-permute-done.1.others, ...), custom_call_target="tpu_custom_call" | custom-call | tf_op jit(solution)/shard_map/pick/pallas_call | solution.py:278
  7.2 0.0 copy-done.1
  7.2 0.0 copy-done.4
  7.2 24.5 %main.1 = bf16[64,1024]{1,0:T(8,128)(2,1)S(1)} custom-call(bf16[64,1024]{1,0:T(8,128)(2,1)S(1)} %copy-done.1, bf16[1024,8192]{1,0:T(8,128)(2,1)} %refs_1_.1, f32[64,128]{1,0:T(8,128)S(1)} %get-tuple-element.7.refs_2_, bf16[8,64,1024]{2,1,0:T(8,128)(2,1)S(1)} %get-tuple-element.8.refs_3_, s32[1,64]{1,0:T(1,128)S(1)} %bitcast.2), custom_call_target="tpu_custom_call" | custom-call | tf_op jit(solution)/shard_map/main/pallas_call | solution.py:304
  31.7 0.7 %copy.9 = bf16[64,1024]{1,0:T(8,128)(2,1)} copy(bf16[64,1024]{1,0:T(8,128)(2,1)S(1)} %main.1) | data formatting | bytes 262144
Async XLA Ops:
  0.0 1.7 %collective-permute-start.1 = (bf16[64,1024]{1,0:T(8,128)(2,1)}, bf16[64,1024]{1,0:T(8,128)(2,1)S(1)}, u32[]{:S(2)}, u32[]{:S(2)}) collective-permute-start(bf16[64,1024]{1,0:T(8,128)(2,1)} %refs_0_.1), channel_id=1, source_target_pairs={{0,8},{8,0},{1,9},{9,1},{2,10},{10,2},{3,11},{11,3},{4,12},{12,4},... | collective-permute-start | bytes 393224 | tf_op jit(solution)/shard_map/ppermute | solution.py:274
  0.5 1.3 %collective-permute-start = (s32[4]{0:T(128)}, s32[4]{0:T(128)S(1)}, u32[]{:S(2)}, u32[]{:S(2)}) collective-permute-start(s32[4]{0:T(128)} %wanted_in.1), channel_id=1, source_target_pairs={{0,8},{8,0},{1,9},{9,1},{2,10},{10,2},{3,11},{11,3},{4,12},{12,4},... | collective-permute-start | bytes 56 | tf_op jit(solution)/shard_map/ppermute | solution.py:273
  1.7 0.9 %copy-start = (bf16[64,1024]{1,0:T(8,128)(2,1)S(1)}, bf16[64,1024]{1,0:T(8,128)(2,1)}, u32[]{:S(2)}) copy-start(bf16[64,1024]{1,0:T(8,128)(2,1)} %refs_0_.1) | copy-start | bytes 393220
  2.6 0.7 %copy-start.2 = (s32[256]{0:T(256)S(1)}, s32[256]{0:T(256)}, u32[]{:S(2)}) copy-start(s32[256]{0:T(256)} %table_in.1) | copy-start | bytes 3076
  3.3 0.7 %copy-start.3 = (s32[4]{0:T(128)S(1)}, s32[4]{0:T(128)}, u32[]{:S(2)}) copy-start(s32[4]{0:T(128)} %wanted_in.1) | copy-start | bytes 52
  4.0 3.2 %copy-start.1 = (bf16[64,1024]{1,0:T(8,128)(2,1)S(1)}, bf16[64,1024]{1,0:T(8,128)(2,1)}, u32[]{:S(2)}) copy-start(bf16[64,1024]{1,0:T(8,128)(2,1)} %refs_0_.1) | copy-start | bytes 393220
  4.0 3.2 %copy-start.4 = (s32[64]{0:T(128)S(1)}, s32[64]{0:T(128)}, u32[]{:S(2)}) copy-start(s32[64]{0:T(128)} %param.13) | copy-start | bytes 772

commit v7 on v5

--- a/solution.py
+++ b/solution.py
@@ -12,7 +12,7 @@
 TAIL = 128
 LEVELS = 32000.0
 ROWS = 16
-USED = (0, 2, 4, 1, 6, 3, 5, 7)
+USED = (0, 2, 4, 6, 1, 3, 5, 7)
 AHEAD = 2
 
 
@@ -198,9 +198,9 @@
     s_sum[...] = shrunk[...] + s_pair[...]
     for i in range(3):
         s_copies.append(send(s_sum, s_in.at[i], s_send.at[i], s_recv.at[i], peers[i]))
+    x_step(2)
+    x_step(3)
     for i in range(3):
-        if i < 2:
-            x_step(i + 2)
         mine = product(2 * i + 1)
         x_copies[i].wait_recv()
         mine = mine + decode(x_in.at[i], width)

time: 31.8 us -> 31.8 us (level)
  no operation moved by 1% of the time
where the time goes in v7:
time: 31.8 us; the launch traced here: 31.6 us
  Pallas kernels  27 us (85%)
  local copies, waits for them, and re-layouts  2.9 us (9%)
  waiting for transfers between devices  1.2 us (4%)
  starting transfers between devices  0.51 us (2%)
    pallas_call x1, Pallas kernels, kernel_shards(): pl.pallas_call(main_kernel, out_shape=jax.ShapeDtypeStruct((rows, width),...  23.8 us
    pallas_call x1, Pallas kernels, kernel_shards(): pl.pallas_call(functools.partial(pick_kernel, owned), out_shape=[jax.Shap...  3.22 us
    unnamed x11, local copies, waits for them, and re-layouts  2.9 us
    ppermute x1, waiting for transfers between devices, kernel_shards(): other_blocks = lax.ppermute(adapter_per_block, 'replica', [(0, 1), (1, 0)])  1.2 us
  transfers between devices with their start and end apart: 2, of which 1 were waited for; matrix products, arithmetic and copies ran while one was open for 0% of the time, Pallas kernels for 0%

profile of v7, /device:TPU:0, one launch (start us, length us, event | category | flops | bytes accessed | tf_op | source)
XLA Modules:
  0.0 31.6 jit_solution(7619509744102245185)
XLA Ops:
  0.0 0.5 %collective-permute-start.1 = (bf16[64,1024]{1,0:T(8,128)(2,1)}, bf16[64,1024]{1,0:T(8,128)(2,1)S(1)}, u32[]{:S(2)}, u32[]{:S(2)}) collective-permute-start(bf16[64,1024]{1,0:T(8,128)(2,1)} %refs_0_.1), channel_id=1, source_target_pairs={{0,8},{8,0},{1,9},{9,1},{2,10},{10,2},{3,11},{11,3},{4,12},{12,4},... | collective-permute-start | bytes 393224 | tf_op jit(solution)/shard_map/ppermute | solution.py:272
  0.5 0.1 collective-permute-start
  0.5 1.2 %collective-permute-done.other_in = s32[4]{0:T(128)S(1)} collective-permute-done((s32[4]{0:T(128)}, s32[4]{0:T(128)S(1)}, u32[]{:S(2)}, u32[]{:S(2)}) %collective-permute-start) | collective-permute-done | bytes 48 | tf_op jit(solution)/shard_map/ppermute | solution.py:271
  1.7 0.0 collective-permute-done.1.others
  1.7 0.0 copy-start
  1.7 0.9 %copy-done = bf16[64,1024]{1,0:T(8,128)(2,1)S(1)} copy-done((bf16[64,1024]{1,0:T(8,128)(2,1)S(1)}, bf16[64,1024]{1,0:T(8,128)(2,1)}, u32[]{:S(2)}) %copy-start) | copy-done | bytes 131096
  2.6 0.0 copy-start.2
  2.6 0.7 %copy-done.2 = s32[256]{0:T(256)S(1)} copy-done((s32[256]{0:T(256)S(1)}, s32[256]{0:T(256)}, u32[]{:S(2)}) %copy-start.2) | copy-done | bytes 1048
  3.3 0.0 copy-start.3
  3.3 0.7 %copy-done.3 = s32[4]{0:T(128)S(1)} copy-done((s32[4]{0:T(128)S(1)}, s32[4]{0:T(128)}, u32[]{:S(2)}) %copy-start.3) | copy-done | bytes 40
  4.0 0.0 copy-start.1
  4.0 0.0 copy-start.4
  4.0 3.2 %pick.1 = (f32[64,128]{1,0:T(8,128)S(1)}, bf16[8,64,1024]{2,1,0:T(8,128)(2,1)S(1)}) custom-call(s32[4]{0:T(128)S(1)} %copy-done.3, s32[4]{0:T(128)S(1)} %collective-permute-done.other_in, s32[256]{0:T(256)S(1)} %copy-done.2, bf16[64,1024]{1,0:T(8,128)(2,1)S(1)} %copy-done, bf16[64,1024]{1,0:T(8,128)(2,1)S(1)} %collective-permute-done.1.others, ...), custom_call_target="tpu_custom_call" | custom-call | tf_op jit(solution)/shard_map/pick/pallas_call | solution.py:276
  7.2 0.0 copy-done.1
  7.2 0.0 copy-done.4
  7.2 23.8 %main.1 = bf16[64,1024]{1,0:T(8,128)(2,1)S(1)} custom-call(bf16[64,1024]{1,0:T(8,128)(2,1)S(1)} %copy-done.1, bf16[1024,8192]{1,0:T(8,128)(2,1)} %refs_1_.1, f32[64,128]{1,0:T(8,128)S(1)} %get-tuple-element.7.refs_2_, bf16[8,64,1024]{2,1,0:T(8,128)(2,1)S(1)} %get-tuple-element.8.refs_3_, s32[1,64]{1,0:T(1,128)S(1)} %bitcast.2), custom_call_target="tpu_custom_call" | custom-call | tf_op jit(solution)/shard_map/main/pallas_call | solution.py:302
  31.0 0.7 %copy.9 = bf16[64,1024]{1,0:T(8,128)(2,1)} copy(bf16[64,1024]{1,0:T(8,128)(2,1)S(1)} %main.1) | data formatting | bytes 262144
Async XLA Ops:
  0.0 1.7 %collective-permute-start.1 = (bf16[64,1024]{1,0:T(8,128)(2,1)}, bf16[64,1024]{1,0:T(8,128)(2,1)S(1)}, u32[]{:S(2)}, u32[]{:S(2)}) collective-permute-start(bf16[64,1024]{1,0:T(8,128)(2,1)} %refs_0_.1), channel_id=1, source_target_pairs={{0,8},{8,0},{1,9},{9,1},{2,10},{10,2},{3,11},{11,3},{4,12},{12,4},... | collective-permute-start | bytes 393224 | tf_op jit(solution)/shard_map/ppermute | solution.py:272
  0.5 1.3 %collective-permute-start = (s32[4]{0:T(128)}, s32[4]{0:T(128)S(1)}, u32[]{:S(2)}, u32[]{:S(2)}) collective-permute-start(s32[4]{0:T(128)} %wanted_in.1), channel_id=1, source_target_pairs={{0,8},{8,0},{1,9},{9,1},{2,10},{10,2},{3,11},{11,3},{4,12},{12,4},... | collective-permute-start | bytes 56 | tf_op jit(solution)/shard_map/ppermute | solution.py:271
  1.7 0.9 %copy-start = (bf16[64,1024]{1,0:T(8,128)(2,1)S(1)}, bf16[64,1024]{1,0:T(8,128)(2,1)}, u32[]{:S(2)}) copy-start(bf16[64,1024]{1,0:T(8,128)(2,1)} %refs_0_.1) | copy-start | bytes 393220
  2.6 0.7 %copy-start.2 = (s32[256]{0:T(256)S(1)}, s32[256]{0:T(256)}, u32[]{:S(2)}) copy-start(s32[256]{0:T(256)} %table_in.1) | copy-start | bytes 3076
  3.3 0.7 %copy-start.3 = (s32[4]{0:T(128)S(1)}, s32[4]{0:T(128)}, u32[]{:S(2)}) copy-start(s32[4]{0:T(128)} %wanted_in.1) | copy-start | bytes 52
  4.0 3.2 %copy-start.1 = (bf16[64,1024]{1,0:T(8,128)(2,1)S(1)}, bf16[64,1024]{1,0:T(8,128)(2,1)}, u32[]{:S(2)}) copy-start(bf16[64,1024]{1,0:T(8,128)(2,1)} %refs_0_.1) | copy-start | bytes 393220
  4.0 3.2 %copy-start.4 = (s32[64]{0:T(128)S(1)}, s32[64]{0:T(128)}, u32[]{:S(2)}) copy-start(s32[64]{0:T(128)} %param.13) | copy-start | bytes 772
